TPU v7x, 32 devices: a whole 2x2x4 slice. The times are simulated.
32 devices in a mesh: seq: 8 (over z, x), grp: 4 (over y, core).
Axes of the slice: x: 2, y: 2, z: 4, core: 2. Of those that a mesh axis runs over, the one named last changes fastest.
Arguments:
- query_rows: bfloat16 [32768, 2048], P(('seq', 'grp')), may hold values from -8 to 8
- key_rows: bfloat16 [32768, 2048], P(('seq', 'grp')), may hold values from -8 to 8
- value_rows: bfloat16 [32768, 2048], P(('seq', 'grp')), may hold values from -6 to 6
- cluster_ids: int32 [8, 32768], P(None, ('seq', 'grp')), may hold values from 0 to 255, as said below
Outputs:
- attended: bfloat16 [32768, 2048], P(('seq', 'grp'))
Inputs may be any that keep to these rules, and one draw needn't show every extreme that they name: `cluster_ids`: in each routed head no cluster is named by more than 6 of one device's 1024 tokens, and in each routed head one cluster is named by exactly 6 tokens of every device.
All inputs are finite; a program needn't handle non-finite values.
Results may differ from a plain program's by a relative error of at most 0.0039.
Values may be sent and summed in bfloat16 or wider, within the bound.
No kernel may reach another device: no remote copies, remote signals or barrier semaphores. Data moves between devices by JAX's collectives and lax.ppermute only.
A program may use at most 192 MiB of HBM per device.

v0:
```python
import jax
import jax.numpy as jnp
from jax import lax
from jax.sharding import PartitionSpec as P

HEADS_L = 8
HEADS_R = 8
HEAD_DIM = 128
WINDOW = 1024
CLUSTERS = 256
CAP = 6


NEGATIVE = -1e30


def from_behind(block, axis, distance):
    devices = range(lax.axis_size(axis))
    route = [(i - distance, i) for i in devices if i - distance in devices]
    return lax.ppermute(block, axis, route)


def shortened(value):
    return jax.tree.map(lambda a: a.astype(jnp.bfloat16) if a.dtype == jnp.float32 else a, value)


def weigh_values(scores, allowed, value_part, equation):
    masked = jnp.where(allowed, scores, NEGATIVE)
    peak_val = jnp.max(masked, axis=-1, keepdims=True)
    weights = jnp.exp(masked - peak_val)
    totals = jnp.sum(weights, axis=-1, keepdims=True)
    mixture = jnp.einsum(
        equation, weights.astype(jnp.bfloat16), value_part, preferred_element_type=jnp.float32
    )
    return (mixture, totals)


def window_heads(query_rows, key_rows, value_rows, my_index):
    shard_len = query_rows.shape[0]
    feat_width = HEADS_L * HEAD_DIM
    score_scale = HEAD_DIM ** (-0.5)
    own_kv = jnp.stack([key_rows[:, :feat_width], value_rows[:, :feat_width]])
    earlier = from_behind(own_kv, ("seq", "grp"), 1)
    joined = jnp.concatenate([earlier, own_kv], axis=1)
    blk_rows = min(512, shard_len)
    pieces = []
    for first_row in range(0, shard_len, blk_rows):
        blk_len = min(blk_rows, shard_len - first_row)
        lower_key = first_row + shard_len - WINDOW
        span_len = WINDOW + blk_len
        query_blk = query_rows[first_row : first_row + blk_len, :feat_width].reshape(
            blk_len, HEADS_L, HEAD_DIM
        )
        key_blk = joined[0, lower_key : lower_key + span_len].reshape(span_len, HEADS_L, HEAD_DIM)
        value_blk = joined[1, lower_key : lower_key + span_len].reshape(span_len, HEADS_L, HEAD_DIM)
        scores = (
            jnp.einsum("qhd,khd->hqk", query_blk, key_blk, preferred_element_type=jnp.float32)
            * score_scale
        )
        row_ids = jnp.arange(blk_len, dtype=jnp.int32)[:, None]
        col_ids = jnp.arange(span_len, dtype=jnp.int32)[None, :]
        offset = WINDOW + row_ids - col_ids
        allowed = (
            (offset >= 0)
            & (offset < WINDOW)
            & (my_index * shard_len + first_row - WINDOW + col_ids >= 0)
        )
        mixture, totals = weigh_values(scores, allowed[None], value_blk, "hqk,khd->qhd")
        result = mixture / jnp.transpose(totals, (1, 0, 2))
        pieces.append(result.astype(jnp.bfloat16).reshape(blk_len, feat_width))
    return jnp.concatenate(pieces, axis=0)


def cluster_attention(routed_rows, routed_slots, shard_len):
    head_count, clus_count, source_count, capacity, feat_len = routed_rows.shape
    slot_total = source_count * capacity
    score_scale = HEAD_DIM ** (-0.5)
    flat_rows = routed_rows.reshape(head_count, clus_count, slot_total, feat_len)
    flat_slots = routed_slots.reshape(head_count, clus_count, slot_total)
    anchor = jnp.arange(slot_total, dtype=jnp.int32) // capacity
    global_pos = jnp.where(flat_slots >= 0, anchor[None, None, :] * shard_len + flat_slots, -1)
    blk_rows = min(512, slot_total)

    def one_head(head_inputs):
        head_rows, head_pos = head_inputs
        key_part = head_rows[:, :, HEAD_DIM : 2 * HEAD_DIM]
        value_part = head_rows[:, :, 2 * HEAD_DIM :]
        pieces = []
        for first_row in range(0, slot_total, blk_rows):
            blk_len = min(blk_rows, slot_total - first_row)
            query_blk = head_rows[:, first_row : first_row + blk_len, :HEAD_DIM]
            scores = (
                jnp.einsum("cqd,ckd->cqk", query_blk, key_part, preferred_element_type=jnp.float32)
                * score_scale
            )
            query_pos = head_pos[:, first_row : first_row + blk_len, None]
            allowed = (head_pos[:, None, :] >= 0) & (head_pos[:, None, :] <= query_pos)
            mixture, totals = weigh_values(scores, allowed, value_part, "cqk,ckd->cqd")
            pieces.append((mixture / totals).astype(jnp.bfloat16))
        return jnp.concatenate(pieces, axis=1)

    outputs = lax.map(one_head, (flat_rows, global_pos))
    return outputs.reshape(head_count, clus_count, source_count, capacity, HEAD_DIM)


def on_device(query_rows, key_rows, value_rows, cluster_ids):
    shard_len = query_rows.shape[0]
    feat_width = HEADS_L * HEAD_DIM
    device_count = lax.axis_size(("seq", "grp"))
    my_index = lax.axis_index(("seq", "grp"))
    clus_dev = CLUSTERS // device_count
    slot_count = CLUSTERS * CAP
    row_ids = jnp.arange(shard_len, dtype=jnp.int32)[:, None]
    col_ids = jnp.arange(shard_len, dtype=jnp.int32)[None, :]
    earlier_same = (cluster_ids[:, :, None] == cluster_ids[:, None, :]) & (col_ids < row_ids)[None]
    slot_rank = jnp.sum(earlier_same, axis=2, dtype=jnp.int32)
    owner = cluster_ids // clus_dev
    member = cluster_ids % clus_dev
    target = (member * device_count + owner) * CAP + slot_rank
    slot_ids = jnp.arange(slot_count, dtype=jnp.int32)
    token_next = jnp.arange(shard_len, dtype=jnp.int32) + 1

    def routed_part(matrix):
        return matrix[:, feat_width:].reshape(shard_len, HEADS_R, HEAD_DIM)

    packed = jnp.concatenate(
        [routed_part(query_rows), routed_part(key_rows), routed_part(value_rows)], axis=2
    )
    row_list = []
    slot_list = []
    for head in range(HEADS_R):
        picks = slot_ids[:, None] == target[head][None, :]
        row_list.append(
            jnp.dot(
                picks.astype(jnp.bfloat16), packed[:, head], preferred_element_type=jnp.float32
            ).astype(jnp.bfloat16)
        )
        slot_list.append(
            jnp.sum(jnp.where(picks, token_next[None, :], 0), axis=1, dtype=jnp.int32) - 1
        )
    send_rows = jnp.stack(row_list)
    send_slots = jnp.stack(slot_list)
    outputs = cluster_attention(
        lax.all_to_all(
            send_rows.reshape(HEADS_R, clus_dev, device_count, CAP, 3 * HEAD_DIM),
            ("seq", "grp"),
            split_axis=2,
            concat_axis=2,
            tiled=True,
        ),
        lax.all_to_all(
            send_slots.reshape(HEADS_R, clus_dev, device_count, CAP),
            ("seq", "grp"),
            split_axis=2,
            concat_axis=2,
            tiled=True,
        ),
        shard_len,
    )
    returned = lax.all_to_all(
        shortened(outputs), ("seq", "grp"), split_axis=2, concat_axis=2, tiled=True
    ).astype(outputs.dtype)
    local_out = window_heads(query_rows, key_rows, value_rows, my_index)
    flat_back = returned.reshape(HEADS_R, slot_count, HEAD_DIM)
    head_outs = []
    for head in range(HEADS_R):
        picks = (slot_ids[:, None] == target[head][None, :]).astype(jnp.bfloat16)
        head_outs.append(
            jnp.einsum(
                "st,sd->td", picks, flat_back[head], preferred_element_type=jnp.float32
            ).astype(jnp.bfloat16)
        )
    routed_out = jnp.concatenate(head_outs, axis=1)
    return jnp.concatenate([local_out, routed_out], axis=1)


def solution(mesh):
    return jax.shard_map(
        on_device,
        mesh=mesh,
        in_specs=(
            P(("seq", "grp"), None),
            P(("seq", "grp"), None),
            P(("seq", "grp"), None),
            P(None, ("seq", "grp")),
        ),
        out_specs=P(("seq", "grp"), None),
        check_vma=False,
    )
```

profile of v0, /device:TPU:24, one launch (start us, length us, event | category | flops | bytes accessed | tf_op | source)
XLA Modules:
  0.0 561.1 jit_solution(9048515608174049978)
XLA Ops:
  0.3 7.6 %convert_reduce_fusion = s32[8,1024]{1,0:T(8,128)S(1)} fusion(s32[8,1024]{1,0:T(8,128)} %param.9, pred[1024,1024]{1,0:T(8,128)(4,1)S(1)} %iota_compare_fusion.24), kind=kLoop, calls=%fused_computation.16 | loop fusion | flops 33546240 | bytes 1114112 | tf_op jit(solution)/shard_map/reduce_sum | solution.py:116
  8.8 7.0 %select_reduce_fusion = (s32[1536]{0:T(1024)S(1)}, s32[1536]{0:T(1024)S(1)}, s32[1536]{0:T(1024)S(1)}, s32[1536]{0:T(1024)S(1)}, s32[1536]{0:T(1024)S(1)}, /*ind...) fusion(s32[1024]{0:T(1024)S(1)} %bitcast.128, s32[1024]{0:T(1024)S(1)} %iota_add_fusion, s32[1024]{0:T(1024)S(1)} %bitcast.146, ...), kind=kLoop, calls=%fused_computation.31 | loop fusion | flops 37736448 | bytes 86016 | tf_op jit(solution)/shard_map/reduce_sum | solution.py:139
  17.1 1.8 copy.163
  19.9 5.9 %all-to-all-start = ((s32[32,1,384]{2,1,0:T(1,128)}), s32[32,1,384]{2,1,0:T(1,128)S(1)}, u32[]{:S(2)}, u32[]{:S(2)}) async-start(s32[32,1,384]{2,1,0:T(1,128)} %reshape.323), calls=%async_computation | async-start | bytes 98304 | tf_op jit(solution)/shard_map/all_to_all | solution.py:151
  25.8 4.0 fusion.89
  29.8 2.6 copy.213
  32.4 4.7 fusion.90
  37.1 4.1 copy.214
  41.2 2.5 copy.212
  43.7 3.8 pad_maximum_fusion
  47.5 2.8 fusion.54
  50.4 2.8 fusion.55
  53.2 2.9 fusion.56
  56.1 2.9 fusion.57
  59.0 2.8 fusion.58
  61.8 1.8 fusion.59
  63.6 15.0 %fusion.60 = bf16[1536,384]{1,0:T(8,128)(2,1)} fusion(s32[1024]{0:T(1024)S(1)} %bitcast.132, bf16[1024,8,384]{0,2,1:T(8,128)(2,1)S(1)} %pad_maximum_fusion), kind=kOutput, calls=%fused_computation.91 | convolution fusion | flops 1210122240 | bytes 1970176 | tf_op jit(solution)/shard_map/dot_general | solution.py:134
  78.6 2.9 fusion.61
  81.5 2.2 stack.51
  85.1 3.3 stack.52
  88.3 3.3 stack.53
  91.6 3.4 stack.54
  95.0 3.3 stack.55
  100.0 2.2 stack.58
  102.3 2.9 constant_dynamic-update-slice_fusion.14
  105.2 2.8 constant_dynamic-update-slice_fusion.13
  110.6 1.4 constant_dynamic-update-slice_fusion.10
  114.7 19.0 %copy.176 = bf16[8,8,32,6,384]{4,1,3,0,2:T(8,128)(2,1)} copy(bf16[8,8,32,6,384]{4,3,2,1,0:T(8,128)(2,1)} %constant_dynamic-update-slice_fusion.8) | data formatting | bytes 18874368 | tf_op jit(solution)/shard_map/stack | solution.py:141
  133.7 5.9 %all-to-all-start.1 = ((bf16[8,8,32,6,384]{4,1,3,0,2:T(8,128)(2,1)}), bf16[8,8,32,6,384]{4,1,3,0,2:T(8,128)(2,1)}, u32[]{:S(2)}, u32[]{:S(2)}) async-start(bf16[8,8,32,6,384]{4,1,3,0,2:T(8,128)(2,1)} %copy.176), calls=%async_computation.1 | async-start | bytes 18874368 | tf_op jit(solution)/shard_map/all_to_all | solution.py:144
  139.6 2.9 copy.208
  142.5 3.9 copy.209
  146.4 4.0 pad_maximum_fusion.1
  150.4 2.0 collective-permute-start
  152.5 2.7 fusion.91
  155.1 2.3 copy.210
  158.8 2.7 fusion.69
  163.6 189.1 %collective-permute-done = bf16[2,1024,1024]{1,2,0:T(8,128)(2,1)} collective-permute-done((bf16[2,1024,1024]{1,2,0:T(8,128)(2,1)}, bf16[2,1024,1024]{1,2,0:T(8,128)(2,1)}, u32[]{:S(2)}, u32[]{:S(2)}) %collective-permute-start) | collective-permute-done | bytes 4194336 | tf_op jit(solution)/shard_map/ppermute | solution.py:20
  352.7 3.7 maximum_maximum_fusion
  356.5 3.4 fusion.88
  359.9 10.7 %fusion.95 = (f32[8,512]{1,0:T(8,128)S(1)}, f32[8,512,1536]{1,2,0:T(8,128)}) fusion(bf16[1536,8,128]{0,2,1:T(8,128)(2,1)S(1)} %bitcast.114, bf16[512,8,128]{0,2,1:T(8,128)(2,1)S(1)} %bitcast.121, pred[512,1536]{0,1:T(8,128)(4,1)S(1)} %copy-done.7), kind=kOutput, calls=%fused_computation.180 | convolution fusion | flops 1629483008 | bytes 30162944 | tf_op jit(solution)/shard_map/qhd,khd->hqk/dot_general | solution.py:57
  370.6 8.2 %copy.177 = bf16[8,8,32,6,384]{4,1,3,2,0:T(8,128)(2,1)} copy(bf16[8,8,32,6,384]{4,1,3,0,2:T(8,128)(2,1)} %all-to-all-done.1) | data formatting | bytes 18874368 | tf_op jit(solution)/shard_map/all_to_all | solution.py:144
  378.8 36.5 %while.10 = (s32[]{:T(128)}, bf16[8,8,192,128]{3,1,2,0:T(8,128)(2,1)}, s32[8,8,192]{2,1,0:T(8,128)S(1)}, bf16[8,8,192,384]{3,1,2,0:T(8,128)(2,1)}, s32[]{:T(128)}) while((s32[]{:T(128)}, bf16[8,8,192,128]{3,1,2,0:T(8,128)(2,1)}, s32[8,8,192]{2,1,0:T(8,128)S(1)}, bf16[8,8,192,384]{3,1,2,0:T(8,128)(2,1)}, s32[]{:T(128)}) %tuple.66), condition=%wide.region_16.17_spmd, body=%wide.region_13.16_spmd.sunk | while | flops 154040832 | bytes 11077701 | solution.py:102
  378.8 1.4 constant_dynamic-slice_fusion.2
  383.4 1.4 constant_dynamic-slice_fusion.2
  387.9 1.4 constant_dynamic-slice_fusion.2
  392.5 1.4 constant_dynamic-slice_fusion.2
  397.1 1.4 constant_dynamic-slice_fusion.2
  401.6 1.4 constant_dynamic-slice_fusion.2
  406.1 1.4 constant_dynamic-slice_fusion.2
  410.7 1.4 constant_dynamic-slice_fusion.2
  415.3 4.5 copy.180
  419.8 47.5 %all-to-all-start.2 = ((bf16[8,8,32,6,128]{4,1,3,0,2:T(8,128)(2,1)}), bf16[8,8,32,6,128]{4,1,3,0,2:T(8,128)(2,1)}, u32[]{:S(2)}, u32[]{:S(2)}) async-start(bf16[8,8,32,6,128]{4,1,3,0,2:T(8,128)(2,1)} %copy.180), calls=%async_computation.2 | async-start | bytes 6291456 | tf_op jit(solution)/shard_map/all_to_all | solution.py:160
  467.3 10.4 %fusion.9 = f32[8,512]{1,0:T(8,128)S(1)} fusion(f32[8,512,1536]{1,2,0:T(8,128)} %get-tuple-element.95, f32[8,512]{1,0:T(8,128)S(1)} %get-tuple-element.94), kind=kLoop, calls=%fused_computation.21 | loop fusion | flops 12578816 | bytes 25198592 | tf_op jit(solution)/shard_map/reduce_sum | solution.py:31
  477.8 13.5 %fusion.63 = bf16[512,8,128]{0,2,1:T(8,128)(2,1)} fusion(bf16[1536,8,128]{0,2,1:T(8,128)(2,1)S(1)} %bitcast.116, f32[8,512,1536]{1,2,0:T(8,128)} %get-tuple-element.95, f32[8,512]{1,0:T(8,128)S(1)} %get-tuple-element.94, f32[512,8]{0,1:T(8,128)S(1)} %bitcast.127), kind=kOutput, calls=%fused_computation.97 | convolution fusion | flops 1624244224 | bytes 29392896 | tf_op jit(solution)/shard_map/hqk,khd->qhd/dot_general | solution.py:32
  491.3 2.3 copy.161
  493.6 12.0 %fusion.94 = (f32[8,512]{1,0:T(8,128)S(1)}, f32[8,512,1536]{1,2,0:T(8,128)}) fusion(bf16[1536,8,128]{0,2,1:T(8,128)(2,1)S(1)} %bitcast.113, bf16[512,8,128]{0,2,1:T(8,128)(2,1)} %bitcast.120, pred[512,1536]{0,1:T(8,128)(4,1)} %get-tuple-element.91), kind=kOutput, calls=%fused_computation.179 | convolution fusion | flops 1629483008 | bytes 30162944 | tf_op jit(solution)/shard_map/qhd,khd->hqk/dot_general | solution.py:57
  505.6 10.3 %fusion.11 = f32[8,512]{1,0:T(8,128)S(1)} fusion(f32[8,512,1536]{1,2,0:T(8,128)} %get-tuple-element.93, f32[8,512]{1,0:T(8,128)S(1)} %get-tuple-element.92), kind=kLoop, calls=%fused_computation.23 | loop fusion | flops 12578816 | bytes 25198592 | tf_op jit(solution)/shard_map/reduce_sum | solution.py:31
  515.9 12.6 %fusion.62 = bf16[512,8,128]{0,2,1:T(8,128)(2,1)S(1)} fusion(bf16[1536,8,128]{0,2,1:T(8,128)(2,1)S(1)} %bitcast.115, f32[8,512,1536]{1,2,0:T(8,128)} %get-tuple-element.93, f32[8,512]{1,0:T(8,128)S(1)} %get-tuple-element.92, f32[512,8]{0,1:T(8,128)S(1)} %bitcast.126), kind=kOutput, calls=%fused_computation.95 | convolution fusion | flops 1624244224 | bytes 29392896 | tf_op jit(solution)/shard_map/hqk,khd->qhd/dot_general | solution.py:32
  529.4 1.5 maximum_dynamic-update-slice_fusion
  530.8 5.4 all-to-all-done.2
  536.3 2.4 fusion.92
  539.6 2.2 fusion.70
  542.3 1.9 fusion.71
  544.7 1.9 fusion.72
  (162 shorter events, 57.0 us)
Async XLA Ops:
  8.7 38.8 %copy-start.13 = (s32[1,1024]{1,0:T(1,128)}, s32[1,1024]{1,0:T(1,128)S(1)}, u32[]{:S(2)}) copy-start(s32[1,1024]{1,0:T(1,128)S(1)} %get-tuple-element.82) | copy-start | bytes 12292
  8.7 41.6 %copy-start.12 = (s32[1,1024]{1,0:T(1,128)}, s32[1,1024]{1,0:T(1,128)S(1)}, u32[]{:S(2)}) copy-start(s32[1,1024]{1,0:T(1,128)S(1)} %get-tuple-element.89) | copy-start | bytes 12292
  8.8 44.5 %copy-start.11 = (s32[1,1024]{1,0:T(1,128)}, s32[1,1024]{1,0:T(1,128)S(1)}, u32[]{:S(2)}) copy-start(s32[1,1024]{1,0:T(1,128)S(1)} %get-tuple-element.88) | copy-start | bytes 12292
  8.8 47.3 %copy-start.9 = (s32[1,1024]{1,0:T(1,128)}, s32[1,1024]{1,0:T(1,128)S(1)}, u32[]{:S(2)}) copy-start(s32[1,1024]{1,0:T(1,128)S(1)} %get-tuple-element.87) | copy-start | bytes 12292
  19.9 113.8 %all-to-all-start = ((s32[32,1,384]{2,1,0:T(1,128)}), s32[32,1,384]{2,1,0:T(1,128)S(1)}, u32[]{:S(2)}, u32[]{:S(2)}) async-start(s32[32,1,384]{2,1,0:T(1,128)} %reshape.323), calls=%async_computation | async-start | bytes 98304 | tf_op jit(solution)/shard_map/all_to_all | solution.py:151
  37.1 4.1 slice-start
  91.6 8.0 %copy-start.8 = (bf16[1536,384]{1,0:T(8,128)(2,1)S(1)}, bf16[1536,384]{1,0:T(8,128)(2,1)}, u32[]{:S(2)}) copy-start(bf16[1536,384]{1,0:T(8,128)(2,1)} %fusion.60) | copy-start | bytes 3538948
  102.3 5.7 %copy-start.4 = (bf16[1,8,32,6,384]{4,3,2,1,0:T(8,128)(2,1)S(1)}, bf16[1,8,32,6,384]{4,3,2,1,0:T(8,128)(2,1)}, u32[]{:S(2)}) copy-start(bf16[1,8,32,6,384]{4,3,2,1,0:T(8,128)(2,1)} %stack.54) | copy-start | bytes 3538948
  102.3 7.0 %copy-start.3 = (bf16[1,8,32,6,384]{4,3,2,1,0:T(8,128)(2,1)S(1)}, bf16[1,8,32,6,384]{4,3,2,1,0:T(8,128)(2,1)}, u32[]{:S(2)}) copy-start(bf16[1,8,32,6,384]{4,3,2,1,0:T(8,128)(2,1)} %stack.55) | copy-start | bytes 3538948
  105.1 5.5 copy-start.2
  133.7 236.9 %all-to-all-start.1 = ((bf16[8,8,32,6,384]{4,1,3,0,2:T(8,128)(2,1)}), bf16[8,8,32,6,384]{4,1,3,0,2:T(8,128)(2,1)}, u32[]{:S(2)}, u32[]{:S(2)}) async-start(bf16[8,8,32,6,384]{4,1,3,0,2:T(8,128)(2,1)} %copy.176), calls=%async_computation.1 | async-start | bytes 18874368 | tf_op jit(solution)/shard_map/all_to_all | solution.py:144
  150.4 202.3 %collective-permute-start = (bf16[2,1024,1024]{1,2,0:T(8,128)(2,1)}, bf16[2,1024,1024]{1,2,0:T(8,128)(2,1)}, u32[]{:S(2)}, u32[]{:S(2)}) collective-permute-start(bf16[2,1024,1024]{1,2,0:T(8,128)(2,1)} %pad_maximum_fusion.1), channel_id=1, source_target_pairs={{0,1},{1,2},{2,3},{3,4},{4,5},{5,6},{6,7},{7,8},{8,9},{9,10},{10,1... | collective-permute-start | bytes 12582920 | tf_op jit(solution)/shard_map/ppermute | solution.py:20
  356.4 3.4 copy-start.5
  356.4 3.4 copy-start.7
  419.8 116.4 %all-to-all-start.2 = ((bf16[8,8,32,6,128]{4,1,3,0,2:T(8,128)(2,1)}), bf16[8,8,32,6,128]{4,1,3,0,2:T(8,128)(2,1)}, u32[]{:S(2)}, u32[]{:S(2)}) async-start(bf16[8,8,32,6,128]{4,1,3,0,2:T(8,128)(2,1)} %copy.180), calls=%async_computation.2 | async-start | bytes 6291456 | tf_op jit(solution)/shard_map/all_to_all | solution.py:160
  467.3 10.4 %copy-start.1 = (bf16[1,1536,1024]{1,2,0:T(8,128)(2,1)S(1)}, bf16[1,1536,1024]{1,2,0:T(8,128)(2,1)}, u32[]{:S(2)}) copy-start(bf16[1,1536,1024]{1,2,0:T(8,128)(2,1)} %get-tuple-element.67) | copy-start | bytes 9437188
  505.6 10.3 %copy-start = (bf16[1,1536,1024]{1,2,0:T(8,128)(2,1)S(1)}, bf16[1,1536,1024]{1,2,0:T(8,128)(2,1)}, u32[]{:S(2)}) copy-start(bf16[1,1536,1024]{1,2,0:T(8,128)(2,1)} %get-tuple-element.66) | copy-start | bytes 9437188
  515.9 13.4 %copy-start.6 = (bf16[512,1024]{1,0:T(8,128)(2,1)S(1)}, bf16[512,1024]{1,0:T(8,128)(2,1)}, u32[]{:S(2)}) copy-start(bf16[512,1024]{1,0:T(8,128)(2,1)} %copy.161) | copy-start | bytes 3145732
  530.8 8.8 %copy-start.14 = (s32[1,1024]{1,0:T(1,128)S(1)}, s32[1,1024]{1,0:T(1,128)}, u32[]{:S(2)}) copy-start(s32[1,1024]{1,0:T(1,128)} %copy-done.13) | copy-start | bytes 12292
  544.5 2.5 copy-start.10
where the time goes:
time: 567 us; the launch traced here: 561 us
  waiting for transfers between devices  195 us (34%)
  local copies, waits for them, and re-layouts  140 us (25%)
  matrix products  109 us (19%)
  starting transfers between devices  61.3 us (11%)
  other arithmetic  55 us (10%)
    ppermute x1, waiting for transfers between devices, from_behind(): return lax.ppermute(block, axis, route)  189 us
    all_to_all x1, starting transfers between devices, on_device(): lax.all_to_all(shortened(outputs), ('seq', 'grp'), split_axis=2, concat_a...  47.5 us
    another operation x10, local copies, waits for them, and re-layouts, on_device(): send_rows = jnp.stack(row_list)  39.7 us
    unnamed x60, local copies, waits for them, and re-layouts  38.6 us
    dot_general x8, matrix products, on_device(): jnp.dot(picks.astype(jnp.bfloat16), packed[:, head], preferred_element_ty...  33.9 us
    dot_general x10, matrix products, weigh_values(): jnp.einsum(equation, weights.astype(jnp.bfloat16), value_part, preferred_...  31 us
    dot_general x2, matrix products, window_heads(): jnp.einsum('qhd,khd->hqk', query_blk, key_blk, preferred_element_type=jnp...  22.7 us
    reduce_sum x10, other arithmetic, weigh_values(): totals = jnp.sum(weights, axis=-1, keepdims=True)  22.7 us
  transfers between devices with their start and end apart: 4, of which 2 were waited for; matrix products, arithmetic and copies ran while one was open for 38% of the time, Pallas kernels for 0%

commit v1 on v0

v1 whole, which is shorter than its diff:
```python
import functools

import jax
import jax.numpy as jnp
from jax import lax
from jax.experimental import pallas as pl
from jax.experimental.pallas import tpu as pltpu
from jax.sharding import PartitionSpec as P

HEADS_L = 8
HEADS_R = 8
HEAD_DIM = 128
WINDOW = 1024
CLUSTERS = 256

RANKS = 8
NEGATIVE = -1e30
AXES = ("seq", "grp")
SCALE = HEAD_DIM ** (-0.5) * 1.4426950408889634
STAT_ROWS = 32
VMEM = 56 * 1024 * 1024


def params(**extra):
    return pltpu.CompilerParams(vmem_limit_bytes=VMEM, **extra)


def contract_last(a, b):
    return lax.dot_general(a, b, (((1,), (1,)), ((), ())), preferred_element_type=jnp.float32)


def iota(shape, dim):
    return lax.broadcasted_iota(jnp.int32, shape, dim)


def as_mask(condition):
    return jnp.where(condition, 1.0, 0.0).astype(jnp.bfloat16)


def rank_kernel(ids_ref, slot_ref, count_ref):
    heads, rows = ids_ref.shape
    before = as_mask(iota((rows, rows), 0) < iota((rows, rows), 1))
    ones = jnp.ones((8, rows), jnp.bfloat16)
    for head in range(heads):
        ids = ids_ref[head : head + 1, :]
        members = as_mask(iota((CLUSTERS, rows), 0) == ids)
        earlier = jnp.dot(members, before, preferred_element_type=jnp.float32)
        rank = jnp.sum(members.astype(jnp.float32) * earlier, axis=0, keepdims=True)
        slot_ref[head : head + 1, :] = ids * RANKS + rank.astype(jnp.int32)
        count_ref[head : head + 1, :] = contract_last(ones, members)[0:1].astype(jnp.int32)


def rank_tokens(cluster_ids):
    heads, rows = cluster_ids.shape
    return pl.pallas_call(
        rank_kernel,
        out_shape=(
            jax.ShapeDtypeStruct((heads, rows), jnp.int32),
            jax.ShapeDtypeStruct((heads, CLUSTERS), jnp.int32),
        ),
        compiler_params=params(),
        name="rank_tokens",
    )(cluster_ids)


def dispatch_kernel(count, slot_ref, *refs):
    sources, outs = refs[:count], refs[count:]
    rows = slot_ref.shape[-1]
    step = 256
    lines = iota((step, rows), 0)

    def body(part, carry):
        base = part * step
        halves = []
        for side in range(2):
            picks = as_mask(lines == slot_ref[0, side : side + 1, :] - base)
            block = jnp.concatenate(
                [s[side].reshape(rows, HEAD_DIM) for s in sources], axis=1
            )
            found = jnp.dot(picks, block, preferred_element_type=jnp.float32)
            halves.append(found.reshape(step // RANKS, RANKS, count * HEAD_DIM))
        joined = jnp.concatenate(halves, axis=1).astype(jnp.bfloat16)
        for i, out in enumerate(outs):
            out[pl.ds(part * (step // RANKS), step // RANKS), 0] = joined[
                :, :, i * HEAD_DIM : (i + 1) * HEAD_DIM
            ]
        return carry

    lax.fori_loop(0, CLUSTERS * RANKS // step, body, 0)


def dispatch(slots, arrays, name):
    devices, rows = slots.shape
    pairs = devices // 2
    in_specs = [pl.BlockSpec((1, 2, rows), lambda i: (i, 0, 0))]
    operands = [slots.reshape(pairs, 2, rows)]
    for array, part in arrays:
        if part is None:
            in_specs.append(pl.BlockSpec((2, rows, HEAD_DIM), lambda i: (i, 0, 0)))
        else:
            in_specs.append(
                pl.BlockSpec((2, 1, rows, HEAD_DIM), lambda i, part=part: (i, part, 0, 0))
            )
        operands.append(array)
    count = len(arrays)
    shape = (CLUSTERS, pairs, 2 * RANKS, HEAD_DIM)
    flops = 2 * devices * rows * CLUSTERS * RANKS * HEAD_DIM * count
    return pl.pallas_call(
        functools.partial(dispatch_kernel, count),
        grid=(pairs,),
        in_specs=in_specs,
        out_specs=[pl.BlockSpec((CLUSTERS, 1, 2 * RANKS, HEAD_DIM), lambda i: (0, i, 0, 0))]
        * count,
        out_shape=[jax.ShapeDtypeStruct(shape, jnp.bfloat16)] * count,
        compiler_params=params(),
        cost_estimate=pl.CostEstimate(
            flops=flops, bytes_accessed=12_000_000 * count, transcendentals=0
        ),
        name=name,
    )(*operands)


def attend_kernel(count, own, bias_ref, own_k, own_v, pair_k, pair_v, *refs):
    queries, outs = refs[:count], refs[count:]
    block, pairs, lines, width = own_k.shape
    slots = pairs * lines
    lane = iota((slots, 2 * slots), 1)
    row = iota((slots, 2 * slots), 0)
    causal = jnp.where((lane <= row) | (lane >= slots), 0.0, NEGATIVE)
    free = jnp.zeros((slots, 2 * slots), jnp.float32)
    causal = jnp.concatenate([causal if own else free] + [free] * (count - 1), axis=0)
    lane = iota((count * slots, 128), 1)

    def read(ref, c):
        return ref[c].reshape(slots, width)

    def one(c):
        keys = jnp.concatenate([read(own_k, c), read(pair_k, c)], axis=0)
        values = jnp.concatenate([read(own_v, c), read(pair_v, c)], axis=0)
        query = jnp.concatenate([read(q, c) for q in queries], axis=0)
        scores = contract_last(query, keys) * SCALE + bias_ref[pl.ds(c, 1), :] + causal
        peak = jnp.max(scores, axis=1, keepdims=True)
        weights = jnp.exp2(scores - peak)
        total = jnp.sum(weights, axis=1, keepdims=True)
        mixture = jnp.dot(
            weights.astype(jnp.bfloat16), values, preferred_element_type=jnp.float32
        )
        mixture = mixture * (1.0 / total)
        level = peak + jnp.log2(total)
        high = level.astype(jnp.bfloat16).astype(jnp.float32)
        rest = level - high
        middle = rest.astype(jnp.bfloat16).astype(jnp.float32)
        stats = jnp.where(lane == 0, high, jnp.where(lane == 1, middle, rest - middle))
        both = jnp.concatenate([mixture, stats], axis=1).astype(jnp.bfloat16)
        for i, out in enumerate(outs):
            out[c] = both[i * slots : (i + 1) * slots].reshape(pairs, lines, 2 * width)

    unroll = 4

    def body(step, carry):
        for j in range(unroll):
            one(step * unroll + j)
        return carry

    lax.fori_loop(0, block // unroll, body, 0)


def attend(bias, own_k, own_v, pair_k, pair_v, queries, own):
    clusters, pairs, lines, width = own_k.shape
    block = 32
    spec = pl.BlockSpec((block, pairs, lines, width), lambda i: (i, 0, 0, 0))
    count = len(queries)
    slots = pairs * lines
    return pl.pallas_call(
        functools.partial(attend_kernel, count, own),
        grid=(clusters // block,),
        in_specs=[pl.BlockSpec((block, 2 * slots), lambda i: (i, 0))] + [spec] * (4 + count),
        out_specs=[pl.BlockSpec((block, pairs, lines, 2 * width), lambda i: (i, 0, 0, 0))]
        * count,
        out_shape=[jax.ShapeDtypeStruct((clusters, pairs, lines, 2 * width), jnp.bfloat16)]
        * count,
        compiler_params=params(),
        cost_estimate=pl.CostEstimate(
            flops=16 * clusters * slots * slots * width * count,
            bytes_accessed=30_000_000,
            transcendentals=0,
        ),
        name="attend_clusters",
    )(bias, own_k, own_v, pair_k, pair_v, *queries)


def collect_kernel(slot_ref, mixed_ref, out_ref, held):
    rows = slot_ref.shape[1]
    clusters, _, lines, width = mixed_ref.shape
    step = 256
    eye = iota((128, 128), 0) == iota((128, 128), 1)
    sub = iota((8, 128), 0)
    for side in range(2):
        wide = mixed_ref[...].reshape(clusters, lines, width).astype(jnp.float32)
        held[...] = (
            wide[:, side * RANKS : (side + 1) * RANKS]
            .reshape(clusters * RANKS, width)
            .astype(jnp.bfloat16)
        )
        levels = jnp.zeros((8, 128), jnp.float32)
        for part in range(rows // step):
            column = slot_ref[0, part * step : (part + 1) * step, side : side + 1]
            picks = as_mask(iota((step, clusters * RANKS), 1) == column)
            found = jnp.dot(picks, held[...], preferred_element_type=jnp.float32)
            out_ref[side, part * step : (part + 1) * step] = found[:, :HEAD_DIM].astype(
                jnp.bfloat16
            )
            stat = found[:, HEAD_DIM : HEAD_DIM + 1] + found[:, HEAD_DIM + 1 : HEAD_DIM + 2]
            stat = stat + found[:, HEAD_DIM + 2 : HEAD_DIM + 3]
            for piece in range(step // 128):
                line = jnp.sum(
                    jnp.where(eye, stat[piece * 128 : (piece + 1) * 128], 0.0),
                    axis=0,
                    keepdims=True,
                )
                levels = jnp.where(sub == part * (step // 128) + piece, line, levels)
        high = levels.astype(jnp.bfloat16).astype(jnp.float32)
        rest = levels - high
        middle = rest.astype(jnp.bfloat16).astype(jnp.float32)
        lines4 = jnp.concatenate(
            [high, middle, rest - middle, jnp.zeros_like(high)], axis=0
        )
        out_ref[side, rows : rows + STAT_ROWS] = lines4.astype(jnp.bfloat16)


def collect(slots, mixed, name):
    devices, rows = slots.shape
    clusters, pairs, lines, width = mixed.shape
    columns = jnp.transpose(slots.reshape(pairs, 2, rows), (0, 2, 1))
    return pl.pallas_call(
        collect_kernel,
        grid=(pairs,),
        in_specs=[
            pl.BlockSpec((1, rows, 2), lambda i: (i, 0, 0)),
            pl.BlockSpec((clusters, 1, lines, width), lambda i: (0, i, 0, 0)),
        ],
        out_specs=pl.BlockSpec((2, rows + STAT_ROWS, HEAD_DIM), lambda i: (i, 0, 0)),
        out_shape=jax.ShapeDtypeStruct((devices, rows + STAT_ROWS, HEAD_DIM), jnp.bfloat16),
        scratch_shapes=[pltpu.VMEM((clusters * RANKS, width), jnp.bfloat16)],
        compiler_params=params(),
        cost_estimate=pl.CostEstimate(
            flops=2 * devices * rows * clusters * RANKS * width,
            bytes_accessed=16_000_000,
            transcendentals=0,
        ),
        name=name,
    )(columns, mixed)


def window_kernel(first_ref, q_ref, own_k, own_v, past_k, past_v, out_ref):
    rows = q_ref.shape[0]
    step = 256
    row = iota((step, step), 0)
    column = iota((step, step), 1)

    def run(with_past):
        for part in range(rows // step):
            query = q_ref[part * step : (part + 1) * step]
            stop = (part + 1) * step
            keys, values = own_k[:stop], own_v[:stop]
            if with_past:
                keys = jnp.concatenate([past_k[part * step :], keys], axis=0)
                values = jnp.concatenate([past_v[part * step :], values], axis=0)
            scores = contract_last(query, keys)
            span = scores.shape[1]
            pieces = []
            if with_past:
                pieces.append(jnp.where(column > row, scores[:, :step], NEGATIVE))
                pieces.append(scores[:, step : span - step])
            elif span > step:
                pieces.append(scores[:, : span - step])
            pieces.append(jnp.where(column <= row, scores[:, span - step :], NEGATIVE))
            scores = jnp.concatenate(pieces, axis=1) if len(pieces) > 1 else pieces[0]
            peak = jnp.max(scores, axis=1, keepdims=True)
            weights = jnp.exp2((scores - peak) * SCALE)
            total = jnp.sum(weights, axis=1, keepdims=True)
            mixture = jnp.dot(
                weights.astype(jnp.bfloat16), values, preferred_element_type=jnp.float32
            )
            out_ref[part * step : (part + 1) * step] = (mixture * (1.0 / total)).astype(
                jnp.bfloat16
            )

    pl.when(first_ref[0] == 0)(lambda: run(False))
    pl.when(first_ref[0] != 0)(lambda: run(True))


def window_heads(my_index, query_rows, key_rows, value_rows, past):
    rows, width = query_rows.shape
    own = pl.BlockSpec((rows, HEAD_DIM), lambda h: (0, h))

    def part(index):
        return pl.BlockSpec((None, rows, HEAD_DIM), lambda h: (index, 0, h))

    return pl.pallas_call(
        window_kernel,
        grid=(HEADS_L,),
        in_specs=[pl.BlockSpec(memory_space=pltpu.SMEM), own, own, own, part(0), part(1)],
        out_specs=own,
        out_shape=jax.ShapeDtypeStruct((rows, width), jnp.bfloat16),
        compiler_params=params(),
        cost_estimate=pl.CostEstimate(
            flops=8 * HEADS_L * rows * 1280 * HEAD_DIM,
            bytes_accessed=14_000_000,
            transcendentals=0,
        ),
        name="window_heads",
    )(my_index.reshape(1), query_rows, key_rows, value_rows, past, past)


def merge_kernel(count, valid_ref, base_ref, *refs):
    del base_ref
    parts, out_ref = refs[:count], refs[count]
    rows = out_ref.shape[0]
    eye = iota((128, 128), 0) == iota((128, 128), 1)
    levels = []
    for i, part in enumerate(parts):
        stats = part[rows : rows + STAT_ROWS].astype(jnp.float32)
        level = stats[0:8] + stats[8:16] + stats[16:24]
        levels.append(jnp.where(valid_ref[i] != 0, level, NEGATIVE))
    peak = functools.reduce(jnp.maximum, levels)
    shares = [jnp.exp2(level - peak) for level in levels]
    whole = functools.reduce(jnp.add, shares)
    shares = [share / whole for share in shares]
    for piece in range(rows // 128):
        here = slice(piece * 128, (piece + 1) * 128)
        result = jnp.zeros((128, HEAD_DIM), jnp.float32)
        for part, share in zip(parts, shares):
            column = jnp.sum(
                jnp.where(eye, share[piece : piece + 1], 0.0), axis=1, keepdims=True
            )
            result = result + part[here].astype(jnp.float32) * column
        out_ref[here] = result.astype(jnp.bfloat16)


def merge(base, parts, valid):
    rows, width = base.shape
    spec = pl.BlockSpec((None, rows + STAT_ROWS, HEAD_DIM), lambda h: (h, 0, 0))
    return pl.pallas_call(
        functools.partial(merge_kernel, len(parts)),
        grid=(HEADS_R,),
        in_specs=[pl.BlockSpec(memory_space=pltpu.SMEM), pl.BlockSpec(memory_space=pl.ANY)]
        + [spec] * len(parts),
        out_specs=pl.BlockSpec((rows, HEAD_DIM), lambda h: (0, HEADS_L + h)),
        out_shape=jax.ShapeDtypeStruct((rows, width), jnp.bfloat16),
        input_output_aliases={1: 0},
        compiler_params=params(),
        name="merge_parts",
    )(valid, base, *parts)


def on_device(query_rows, key_rows, value_rows, cluster_ids):
    rows = query_rows.shape[0]
    local_width = HEADS_L * HEAD_DIM
    device_count = lax.axis_size(AXES)
    my_index = lax.axis_index(AXES)
    group = HEADS_R
    planes = device_count // group
    couples = planes // 2
    plane = my_index // group
    groups = [[group * i + j for j in range(group)] for i in range(planes)]

    def swap(array):
        return lax.all_to_all(
            array, AXES, split_axis=0, concat_axis=0, tiled=True, axis_index_groups=groups
        )

    def move(array, routes):
        pairs = [(group * a + j, group * b + j) for a, b in routes for j in range(group)]
        return lax.ppermute(array, AXES, pairs)

    def heads_first(matrix):
        routed = matrix[:, local_width:].reshape(rows, HEADS_R, HEAD_DIM)
        return jnp.transpose(routed, (1, 0, 2))

    swapped = swap(
        jnp.stack([heads_first(m) for m in (query_rows, key_rows, value_rows)], axis=1)
    )
    slots, counts = rank_tokens(cluster_ids)
    facts = lax.all_gather(jnp.concatenate([slots, counts], axis=1), AXES)
    facts = lax.dynamic_index_in_dim(facts, my_index % group, 1, keepdims=False)
    facts = facts.reshape(planes, group, rows + CLUSTERS)

    def slots_of(index):
        return lax.dynamic_index_in_dim(facts, index, 0, keepdims=False)[:, :rows]

    def bias_of(index):
        held = lax.dynamic_index_in_dim(facts, index, 0, keepdims=False)[:, rows:]
        filled = jnp.arange(RANKS, dtype=jnp.int32)[None, None, :] < held.T[:, :, None]
        return jnp.where(filled, 0.0, NEGATIVE).reshape(CLUSTERS, group * RANKS)

    partner = plane ^ 1
    is_odd = plane % 2 == 1
    pair_rows = move(swapped[:, 1:], [(2 * j, 2 * j + 1) for j in range(couples)])
    queries = swapped[:, 0]

    def visit(queries, shift):
        found = []
        for side in range(2):
            routes = [(2 * j + side, 2 * (j - shift) + 1) for j in range(shift, couples)]
            found.append(move(queries, routes))
        return found

    visitors = visit(queries, 1) if couples > 1 else []
    past = lax.ppermute(
        jnp.stack([key_rows[:, :local_width], value_rows[:, :local_width]]),
        AXES,
        [(i, i + 1) for i in range(device_count - 1)],
    )

    own_q, own_k, own_v = dispatch(
        slots_of(plane), [(swapped, 0), (swapped, 1), (swapped, 2)], "dispatch_own"
    )
    pair_k, pair_v = dispatch(slots_of(partner), [(pair_rows, 0), (pair_rows, 1)], "dispatch_pair")
    bias = jnp.concatenate(
        [bias_of(plane), jnp.where(is_odd, bias_of(partner), NEGATIVE)], axis=1
    )

    def visit_slots(shift):
        homes = [2 * (plane // 2 + shift) + side for side in range(2)]
        return [slots_of(jnp.minimum(home, planes - 1)) for home in homes]

    def give_back(mixed, slots, shift):
        back = []
        for side in range(2):
            found = collect(slots[side], mixed[side], "collect_visit")
            routes = [(2 * (j - shift) + 1, 2 * j + side) for j in range(shift, couples)]
            back.append(move(found, routes))
        return swap(jnp.where(is_odd, back[1], back[0]))

    kept = (bias, own_k, own_v, pair_k, pair_v)
    asked = [own_q]
    homes = visit_slots(1)
    for side, moved in enumerate(visitors):
        asked += dispatch(homes[side], [(moved, None)], "dispatch_visit")
    mixed = attend(*kept, asked, True)
    parts = [swap(collect(slots_of(plane), mixed[0], "collect_own"))]
    if couples > 1:
        parts.append(give_back(mixed[1:], homes, 1))
    for shift in range(2, couples):
        queries, parts[-1] = lax.optimization_barrier((queries, parts[-1]))
        homes = visit_slots(shift)
        asked = []
        for side, moved in enumerate(visit(queries, shift)):
            asked += dispatch(homes[side], [(moved, None)], "dispatch_visit")
        parts.append(give_back(attend(*kept, asked, False), homes, shift))
    valid = [jnp.int32(1)] + [(plane // 2 >= s).astype(jnp.int32) for s in range(1, couples)]
    local_out = window_heads(my_index, query_rows, key_rows, value_rows, past)
    return merge(local_out, parts, jnp.stack(valid))


def solution(mesh):
    return jax.shard_map(
        on_device,
        mesh=mesh,
        in_specs=(P(AXES, None), P(AXES, None), P(AXES, None), P(None, AXES)),
        out_specs=P(AXES, None),
        check_vma=False,
    )
```

time: 567 us -> 501 us (0.88)
  the two profiles are of different devices: /device:TPU:24 before, /device:TPU:16 now
where the time goes in v1:
time: 501 us; the launch traced here: 500 us
  Pallas kernels  215 us (43%)
  waiting for transfers between devices  188 us (38%)
  local copies, waits for them, and re-layouts  40.8 us (8%)
  starting transfers between devices  28.4 us (6%)
  other arithmetic  14.5 us (3%)
  between operations  13.7 us (3%)
    ppermute x5, waiting for transfers between devices, move(): return lax.ppermute(array, AXES, pairs)  118 us
    pallas_call x4, Pallas kernels, dispatch(): pl.pallas_call(functools.partial(dispatch_kernel, count), grid=(pairs,),...  74.3 us
    all_to_all x3, waiting for transfers between devices, swap(): lax.all_to_all(array, AXES, split_axis=0, concat_axis=0, tiled=True, axis...  69.8 us
    pallas_call x1, Pallas kernels, attend(): pl.pallas_call(functools.partial(attend_kernel, count, own), grid=(cluste...  65 us
    pallas_call x3, Pallas kernels, collect(): pl.pallas_call(collect_kernel, grid=(pairs,), in_specs=[pl.BlockSpec((1,...  39.4 us
    pallas_call x1, Pallas kernels, window_heads(): pl.pallas_call(window_kernel, grid=(HEADS_L,), in_specs=[pl.BlockSpec(mem...  21.8 us
    ppermute x5, starting transfers between devices, move(): return lax.ppermute(array, AXES, pairs)  13.5 us
    all_to_all x3, starting transfers between devices, swap(): lax.all_to_all(array, AXES, split_axis=0, concat_axis=0, tiled=True, axis...  13 us
  transfers between devices with their start and end apart: 10, of which 4 were waited for; matrix products, arithmetic and copies ran while one was open for 5% of the time, Pallas kernels for 42%

profile of v1, /device:TPU:16, one launch (start us, length us, event | category | flops | bytes accessed | tf_op | source)
XLA Modules:
  0.0 499.8 jit_solution(14643016993276495876)
XLA Ops:
  6.5 5.7 %fusion = (bf16[1024,1024]{1,0:T(8,128)(2,1)}, bf16[1,1024,1024]{2,1,0:T(8,128)(2,1)}, bf16[1,1024,1024]{2,1,0:T(8,128)(2,1)}, bf16[1024,1024]{1,0:T(8,128)(2,1)S(1)}) fusion(bf16[1024,2048]{1,0:T(8,128)(2,1)} %own_k.1, bf16[1024,2048]{1,0:T(8,128)(2,1)} %own_v.1), kind=kLoop, calls=%fused_computation.21 | loop fusion | bytes 16777216 | tf_op jit(solution)/shard_map/slice | solution.py:378
  12.2 4.0 copy.44
  16.2 2.5 copy.45
  18.7 0.0 slice-start
  18.7 1.6 slice-done
  20.3 2.7 copy.43
  23.0 6.2 %pad_maximum_fusion = bf16[8,3,1024,128]{2,3,0,1:T(8,128)(2,1)} fusion(bf16[8,1,1024,128]{2,3,0,1:T(8,128)(2,1)} %bitcast.49, bf16[8,1,1024,128]{2,3,0,1:T(8,128)(2,1)} %bitcast.48, bf16[8,1,1024,128]{2,3,0,1:T(8,128)(2,1)} %bitcast.50), kind=kLoop, calls=%fused_computation | loop fusion | flops 6291456 | bytes 12582912 | tf_op jit(solution)/shard_map/stack | solution.py:382
  29.2 8.6 %copy.38 = bf16[8,3,1024,128]{3,2,1,0:T(8,128)(2,1)} copy(bf16[8,3,1024,128]{2,3,0,1:T(8,128)(2,1)} %pad_maximum_fusion) | data formatting | bytes 12582912 | tf_op jit(solution)/shard_map/stack | solution.py:382
  37.8 4.8 all-to-all-start
  42.6 0.0 all-gather.3.cloned.1.call-start
  42.6 6.9 %rank_tokens.1 = (s32[8,1024]{1,0:T(8,128)}, s32[8,256]{1,0:T(8,128)}) custom-call(s32[8,1024]{1,0:T(8,128)} %ids_ref.1), custom_call_target="tpu_custom_call" | custom-call | tf_op jit(solution)/shard_map/rank_tokens/pallas_call | solution.py:55
  49.5 1.4 pad_add_fusion
  50.9 0.0 all-gather.3.cloned.1.call-update
  50.9 0.0 copy-start.1
  50.9 66.0 %all-to-all-done.refs_0_.refs_1_.refs_2_ = bf16[8,3,1024,128]{3,2,1,0:T(8,128)(2,1)} async-done(((bf16[8,3,1024,128]{3,2,1,0:T(8,128)(2,1)}), bf16[8,3,1024,128]{3,2,1,0:T(8,128)(2,1)}, u32[]{:S(2)}, u32[]{:S(2)}) %all-to-all-start) | async-done | bytes 6291488 | tf_op jit(solution)/shard_map/all_to_all | solution.py:369
  116.9 4.8 slice.57
  121.8 5.5 %collective-permute-start.1 = (bf16[8,2,1024,128]{3,2,1,0:T(8,128)(2,1)}, bf16[8,2,1024,128]{3,2,1,0:T(8,128)(2,1)}, u32[]{:S(2)}, u32[]{:S(2)}) collective-permute-start(bf16[8,2,1024,128]{3,2,1,0:T(8,128)(2,1)} %slice.57), channel_id=1, source_target_pairs={{0,8},{1,9},{2,10},{3,11},{4,12},{5,13},{6,14},{7,15},{16,24},{17,... | collective-permute-start | bytes 12582920 | tf_op jit(solution)/shard_map/ppermute | solution.py:375
  127.3 0.0 copy-done.1
  127.3 0.0 copy-done.2
  127.3 2.4 pad_maximum_fusion.1
  129.7 1.9 collective-permute-start
  131.7 0.1 lt.71
  131.8 1.4 constant_dynamic-slice_fusion
  133.3 1.7 slice_bitcast_fusion
  135.0 2.6 collective-permute-start.2
  137.7 0.6 reshape.45.slot_ref
  138.3 0.6 reshape.41.slot_ref
  139.0 0.0 copy-start.5
  139.0 0.0 copy-start.4
  139.0 0.1 copy.33
  139.1 2.0 collective-permute-start.3
  141.2 0.1 copy.34
  141.2 2.0 copy.40
  143.2 2.0 copy.41
  145.3 0.0 copy-done.5
  145.3 0.0 copy-done.4
  145.3 0.7 pad_maximum_fusion.2.bias_ref
  146.0 25.9 %dispatch_own.1 = (bf16[256,4,16,128]{3,2,1,0:T(8,128)(2,1)}, bf16[256,4,16,128]{3,2,1,0:T(8,128)(2,1)}, bf16[256,4,16,128]{3,2,1,0:T(8,128)(2,1)}) custom-call(s32[4,2,1024]{2,1,0:T(2,128)} %reshape.41.slot_ref, bf16[8,3,1024,128]{3,2,1,0:T(8,128)(2,1)} %all-to-all-done.refs_0_.refs_1_.refs_2_, ...), custom_call_target="tpu_custom_call" | custom-call | flops 12884901888 | bytes 36000000 | tf_op jit(solution)/shard_map/dispatch_own/pallas_call | solution.py:108
  171.9 54.8 %collective-permute-done.2.refs_0_ = bf16[8,1024,128]{2,1,0:T(8,128)(2,1)} collective-permute-done((bf16[8,1024,128]{2,1,0:T(8,128)(2,1)S(1)}, bf16[8,1024,128]{2,1,0:T(8,128)(2,1)}, u32[]{:S(2)}, u32[]{:S(2)}) %collective-permute-start.2) | collective-permute-done | bytes 2097184 | tf_op jit(solution)/shard_map/ppermute | solution.py:375
  226.7 15.8 %dispatch_visit.2.refs_1_ = bf16[256,4,16,128]{3,2,1,0:T(8,128)(2,1)} custom-call(s32[4,2,1024]{2,1,0:T(2,128)} %copy-done.5, bf16[8,1024,128]{2,1,0:T(8,128)(2,1)} %collective-permute-done.2.refs_0_), custom_call_target="tpu_custom_call" | custom-call | flops 4294967296 | bytes 12000000 | tf_op jit(solution)/shard_map/dispatch_visit/pallas_call | solution.py:108
  242.4 0.0 collective-permute-done.3.refs_0_
  242.5 15.8 %dispatch_visit.3.refs_2_ = bf16[256,4,16,128]{3,2,1,0:T(8,128)(2,1)} custom-call(s32[4,2,1024]{2,1,0:T(2,128)} %copy-done.4, bf16[8,1024,128]{2,1,0:T(8,128)(2,1)} %collective-permute-done.3.refs_0_), custom_call_target="tpu_custom_call" | custom-call | flops 4294967296 | bytes 12000000 | tf_op jit(solution)/shard_map/dispatch_visit/pallas_call | solution.py:108
  258.3 0.0 collective-permute-done.1.refs_0_.refs_1_
  258.3 16.8 %dispatch_pair.1 = (bf16[256,4,16,128]{3,2,1,0:T(8,128)(2,1)}, bf16[256,4,16,128]{3,2,1,0:T(8,128)(2,1)}) custom-call(s32[4,2,1024]{2,1,0:T(2,128)} %reshape.45.slot_ref, bf16[8,2,1024,128]{3,2,1,0:T(8,128)(2,1)} %collective-permute-done.1.refs_0_.refs_1_, bf16[8,2,1024,128]{3,2,1,0:T(8,128)(2,1)} %collective-permute-done.1.refs_0_.refs_1_), custom_call_target="tpu_custom_call" | custom-call | flops 8589934592 | bytes 24000000 | tf_op jit(solution)/shard_map/dispatch_pair/pallas_call | solution.py:108
  275.1 65.0 %attend_clusters.1 = (bf16[256,4,16,256]{3,2,1,0:T(8,128)(2,1)}, bf16[256,4,16,256]{3,2,1,0:T(8,128)(2,1)}, bf16[256,4,16,256]{3,2,1,0:T(8,128)(2,1)}) custom-call(f32[256,128]{1,0:T(8,128)} %pad_maximum_fusion.2.bias_ref, bf16[256,4,16,128]{3,2,1,0:T(8,128)(2,1)} %get-tuple-element.17.own_k, bf16[256,4,16,128]{3,2,1,0:T(8,128)(2,1)} %get-tuple-element.18.own_v, ...), custom_call_target="tpu_custom_call" | custom-call | flops 6442450944 | bytes 30000000 | tf_op jit(solution)/shard_map/attend_clusters/pallas_call | solution.py:174
  340.1 13.2 %collect_visit.2 = bf16[8,1056,128]{2,1,0:T(8,128)(2,1)} custom-call(s32[4,1024,2]{2,1,0:T(8,128)} %bitcast.52, bf16[256,4,16,256]{3,2,1,0:T(8,128)(2,1)} %get-tuple-element.23.mixed_ref), custom_call_target="tpu_custom_call" | custom-call | flops 8589934592 | bytes 16000000 | tf_op jit(solution)/shard_map/collect_visit/pallas_call | solution.py:235
  353.3 2.0 collective-permute-start.4
  355.3 13.1 %collect_visit.3 = bf16[8,1056,128]{2,1,0:T(8,128)(2,1)} custom-call(s32[4,1024,2]{2,1,0:T(8,128)} %bitcast.51, bf16[256,4,16,256]{3,2,1,0:T(8,128)(2,1)} %get-tuple-element.24.mixed_ref), custom_call_target="tpu_custom_call" | custom-call | flops 8589934592 | bytes 16000000 | tf_op jit(solution)/shard_map/collect_visit/pallas_call | solution.py:235
  368.5 1.3 collective-permute-start.5
  369.8 0.0 copy-done.3
  369.8 2.0 copy.32
  371.8 13.1 %collect_own.1 = bf16[8,1056,128]{2,1,0:T(8,128)(2,1)} custom-call(s32[4,1024,2]{2,1,0:T(8,128)} %bitcast.53, bf16[256,4,16,256]{3,2,1,0:T(8,128)(2,1)} %get-tuple-element.22.mixed_ref), custom_call_target="tpu_custom_call" | custom-call | flops 8589934592 | bytes 16000000 | tf_op jit(solution)/shard_map/collect_own/pallas_call | solution.py:235
  384.9 3.6 all-to-all-start.1
  388.5 0.0 collective-permute-done.4
  388.5 63.1 %collective-permute-done.5 = bf16[8,1056,128]{2,1,0:T(8,128)(2,1)} collective-permute-done((bf16[8,1056,128]{2,1,0:T(8,128)(2,1)}, bf16[8,1056,128]{2,1,0:T(8,128)(2,1)}, u32[]{:S(2)}, u32[]{:S(2)}) %collective-permute-start.5) | collective-permute-done | bytes 2162720 | tf_op jit(solution)/shard_map/ppermute | solution.py:375
  451.6 3.2 broadcast_select_fusion
  454.8 0.0 all-to-all-done.1.refs_0_
  454.8 4.6 all-to-all-start.2
  459.4 0.0 copy-done
  459.4 0.6 add_convert_fusion.valid_ref
  460.1 0.0 collective-permute-done.past_k.past_v
  460.1 21.8 %window_heads.1.base_ref = bf16[1024,2048]{1,0:T(8,128)(2,1)} custom-call(s32[1]{0:T(128)} %bitcast.1.first_ref, bf16[1024,2048]{1,0:T(8,128)(2,1)} %q_ref.1, bf16[1024,2048]{1,0:T(8,128)(2,1)} %own_k.1, bf16[1024,2048]{1,0:T(8,128)(2,1)} %own_v.1, bf16[2,1024,1024]{2,1,0:T(8,128)(2,1)} %collective-permute-done.past_k.past_v, ...), custom_call_target="tpu_custom_call" | custom-call | flops 10737418240 | bytes 14000000 | tf_op jit(solution)/shard_map/window_heads/pallas_call | solution.py:300
  481.8 3.8 all-to-all-done.2.refs_1_
  485.6 7.4 %merge_parts.1 = bf16[1024,2048]{1,0:T(8,128)(2,1)} custom-call(s32[2]{0:T(128)} %add_convert_fusion.valid_ref, bf16[1024,2048]{1,0:T(8,128)(2,1)} %window_heads.1.base_ref, bf16[8,1056,128]{2,1,0:T(8,128)(2,1)} %copy-done, bf16[8,1056,128]{2,1,0:T(8,128)(2,1)} %all-to-all-done.2.refs_1_), custom_call_target="tpu_custom_call", output_to_operand_aliasing={{}: (1, {})} | custom-call | tf_op jit(solution)/shard_map/merge_parts/pallas_call | solution.py:344
  (17 shorter events, 0.1 us)
Async XLA Ops:
  18.7 1.6 slice-start
  37.8 79.1 %all-to-all-start = ((bf16[8,3,1024,128]{3,2,1,0:T(8,128)(2,1)}), bf16[8,3,1024,128]{3,2,1,0:T(8,128)(2,1)}, u32[]{:S(2)}, u32[]{:S(2)}) async-start(bf16[8,3,1024,128]{3,2,1,0:T(8,128)(2,1)} %copy.38), calls=%async_computation | async-start | bytes 12582912 | tf_op jit(solution)/shard_map/all_to_all | solution.py:369
  42.6 89.2 %all-gather.3.cloned.1.call-start = ((), (), s32[]{:S(2)}) async-start(), calls=%async_computation.3 | async-start | bytes 1351680 | tf_op jit(solution)/shard_map/all_gather | solution.py:385
  50.9 76.4 %copy-start.1 = (bf16[1,1024,1024]{2,1,0:T(8,128)(2,1)S(1)}, bf16[1,1024,1024]{2,1,0:T(8,128)(2,1)}, u32[]{:S(2)}) copy-start(bf16[1,1024,1024]{2,1,0:T(8,128)(2,1)} %get-tuple-element.26) | copy-start | bytes 6291460
  116.9 10.4 %copy-start.2 = (bf16[1,1024,1024]{2,1,0:T(8,128)(2,1)S(1)}, bf16[1,1024,1024]{2,1,0:T(8,128)(2,1)}, u32[]{:S(2)}) copy-start(bf16[1,1024,1024]{2,1,0:T(8,128)(2,1)} %get-tuple-element.35) | copy-start | bytes 6291460
  121.8 136.5 %collective-permute-start.1 = (bf16[8,2,1024,128]{3,2,1,0:T(8,128)(2,1)}, bf16[8,2,1024,128]{3,2,1,0:T(8,128)(2,1)}, u32[]{:S(2)}, u32[]{:S(2)}) collective-permute-start(bf16[8,2,1024,128]{3,2,1,0:T(8,128)(2,1)} %slice.57), channel_id=1, source_target_pairs={{0,8},{1,9},{2,10},{3,11},{4,12},{5,13},{6,14},{7,15},{16,24},{17,... | collective-permute-start | bytes 12582920 | tf_op jit(solution)/shard_map/ppermute | solution.py:375
  129.7 330.4 %collective-permute-start = (bf16[2,1024,1024]{2,1,0:T(8,128)(2,1)}, bf16[2,1024,1024]{2,1,0:T(8,128)(2,1)}, u32[]{:S(2)}, u32[]{:S(2)}) collective-permute-start(bf16[2,1024,1024]{2,1,0:T(8,128)(2,1)} %pad_maximum_fusion.1), channel_id=1, source_target_pairs={{0,1},{1,2},{2,3},{3,4},{4,5},{5,6},{6,7},{7,8},{8,9},{9,10},{10,1... | collective-permute-start | bytes 12582920 | tf_op jit(solution)/shard_map/ppermute | solution.py:410
  135.0 91.7 %collective-permute-start.2 = (bf16[8,1024,128]{2,1,0:T(8,128)(2,1)S(1)}, bf16[8,1024,128]{2,1,0:T(8,128)(2,1)}, u32[]{:S(2)}, u32[]{:S(2)}) collective-permute-start(bf16[8,1024,128]{2,1,0:T(8,128)(2,1)S(1)} %slice_bitcast_fusion), channel_id=1, source_target_pairs={{16,8},{17,9},{18,10},{19,11},{20,12},{21,13},{22,14},{23,15}} | collective-permute-start | bytes 6291464 | tf_op jit(solution)/shard_map/ppermute | solution.py:375
  139.0 6.3 %copy-start.5 = (s32[4,2,1024]{2,1,0:T(2,128)}, s32[4,2,1024]{2,1,0:T(2,128)S(1)}, u32[]{:S(2)}) copy-start(s32[4,2,1024]{2,1,0:T(2,128)S(1)} %reshape.46.slot_ref) | copy-start | bytes 98308
  139.0 6.3 %copy-start.4 = (s32[4,2,1024]{2,1,0:T(2,128)}, s32[4,2,1024]{2,1,0:T(2,128)S(1)}, u32[]{:S(2)}) copy-start(s32[4,2,1024]{2,1,0:T(2,128)S(1)} %reshape.47.slot_ref) | copy-start | bytes 98308
  139.1 103.3 %collective-permute-start.3 = (bf16[8,1024,128]{2,1,0:T(8,128)(2,1)S(1)}, bf16[8,1024,128]{2,1,0:T(8,128)(2,1)}, u32[]{:S(2)}, u32[]{:S(2)}) collective-permute-start(bf16[8,1024,128]{2,1,0:T(8,128)(2,1)S(1)} %slice_bitcast_fusion), channel_id=1, source_target_pairs={{24,8},{25,9},{26,10},{27,11},{28,12},{29,13},{30,14},{31,15}} | collective-permute-start | bytes 6291464 | tf_op jit(solution)/shard_map/ppermute | solution.py:375
  353.3 35.2 %collective-permute-start.4 = (bf16[8,1056,128]{2,1,0:T(8,128)(2,1)}, bf16[8,1056,128]{2,1,0:T(8,128)(2,1)}, u32[]{:S(2)}, u32[]{:S(2)}) collective-permute-start(bf16[8,1056,128]{2,1,0:T(8,128)(2,1)} %collect_visit.2), channel_id=1, source_target_pairs={{8,24},{9,25},{10,26},{11,27},{12,28},{13,29},{14,30},{15,31}} | collective-permute-start | bytes 6488072 | tf_op jit(solution)/shard_map/ppermute | solution.py:375
  355.3 14.4 %copy-start.3 = (s32[4,2,1024]{2,1,0:T(2,128)S(1)}, s32[4,2,1024]{2,1,0:T(2,128)}, u32[]{:S(2)}) copy-start(s32[4,2,1024]{2,1,0:T(2,128)} %reshape.41.slot_ref) | copy-start | bytes 98308
  368.5 83.2 %collective-permute-start.5 = (bf16[8,1056,128]{2,1,0:T(8,128)(2,1)}, bf16[8,1056,128]{2,1,0:T(8,128)(2,1)}, u32[]{:S(2)}, u32[]{:S(2)}) collective-permute-start(bf16[8,1056,128]{2,1,0:T(8,128)(2,1)} %collect_visit.3), channel_id=1, source_target_pairs={{8,16},{9,17},{10,18},{11,19},{12,20},{13,21},{14,22},{15,23}} | collective-permute-start | bytes 6488072 | tf_op jit(solution)/shard_map/ppermute | solution.py:375
  384.9 69.9 %all-to-all-start.1 = ((bf16[8,1056,128]{2,1,0:T(8,128)(2,1)}), bf16[8,1056,128]{2,1,0:T(8,128)(2,1)S(1)}, u32[]{:S(2)}, u32[]{:S(2)}) async-start(bf16[8,1056,128]{2,1,0:T(8,128)(2,1)} %collect_own.1), calls=%async_computation.1 | async-start | bytes 4325376 | tf_op jit(solution)/shard_map/all_to_all | solution.py:369
  454.8 4.6 copy-start
  454.8 30.8 %all-to-all-start.2 = ((bf16[8,1056,128]{2,1,0:T(8,128)(2,1)}), bf16[8,1056,128]{2,1,0:T(8,128)(2,1)}, u32[]{:S(2)}, u32[]{:S(2)}) async-start(bf16[8,1056,128]{2,1,0:T(8,128)(2,1)} %broadcast_select_fusion), calls=%async_computation.2 | async-start | bytes 4325376 | tf_op jit(solution)/shard_map/all_to_all | solution.py:369
Sparse Core Ops, SparseCore 0:
  51.0 72.6 all-gather.2

commit v2 on v1

v2 whole, which is shorter than its diff:
```python
import functools

import jax
import jax.numpy as jnp
from jax import lax
from jax.experimental import pallas as pl
from jax.experimental.pallas import tpu as pltpu
from jax.sharding import PartitionSpec as P

HEADS_L = 8
HEADS_R = 8
HEAD_DIM = 128
WINDOW = 1024
CLUSTERS = 256

RANKS = 8
NEGATIVE = -(2.0**100)
AXES = ("seq", "grp")
SCALE = HEAD_DIM ** (-0.5) * 1.4426950408889634
STAT_ROWS = 16
HALVES = 2
VMEM = 56 * 1024 * 1024


def params(**extra):
    return pltpu.CompilerParams(vmem_limit_bytes=VMEM, **extra)


def contract_last(a, b):
    return lax.dot_general(a, b, (((1,), (1,)), ((), ())), preferred_element_type=jnp.float32)


def iota(shape, dim):
    return lax.broadcasted_iota(jnp.int32, shape, dim)


def as_mask(condition):
    return jnp.where(condition, 1.0, 0.0).astype(jnp.bfloat16)


def rank_kernel(ids_ref, slot_ref, count_ref):
    heads, rows = ids_ref.shape
    before = as_mask(iota((rows, rows), 0) < iota((rows, rows), 1))
    ones = jnp.ones((8, rows), jnp.bfloat16)
    for head in range(heads):
        ids = ids_ref[head : head + 1, :]
        members = as_mask(iota((CLUSTERS, rows), 0) == ids)
        earlier = jnp.dot(members, before, preferred_element_type=jnp.float32)
        rank = jnp.sum(members.astype(jnp.float32) * earlier, axis=0, keepdims=True)
        slot_ref[head : head + 1, :] = ids * RANKS + rank.astype(jnp.int32)
        count_ref[head : head + 1, :] = contract_last(ones, members)[0:1].astype(jnp.int32)


def rank_tokens(cluster_ids):
    heads, rows = cluster_ids.shape
    return pl.pallas_call(
        rank_kernel,
        out_shape=(
            jax.ShapeDtypeStruct((heads, rows), jnp.int32),
            jax.ShapeDtypeStruct((heads, CLUSTERS), jnp.int32),
        ),
        compiler_params=params(),
        name="rank_tokens",
    )(cluster_ids)


def near(ids, base, step):
    here = ids - base
    return jnp.where((here >= 0) & (here < step), here, -1).astype(jnp.float32).astype(jnp.bfloat16)


def equal_mask(a, b):
    one, zero = jnp.bfloat16(1.0), jnp.bfloat16(0.0)
    return jnp.where(a == b, one, zero)


def dispatch_rows(slot_ref, read, outs):
    rows = slot_ref.shape[-1]
    fine = 256
    step = 1024
    lines = iota((fine, rows), 0).astype(jnp.float32).astype(jnp.bfloat16)

    def body(part, carry):
        base = part * step
        halves = []
        for side in range(2):
            ids = slot_ref[0, side : side + 1, :]
            picks = jnp.concatenate(
                [
                    equal_mask(
                        lines, jnp.broadcast_to(near(ids, base + i, fine), (fine, rows))
                    )
                    for i in range(0, step, fine)
                ],
                axis=0,
            )
            found = jnp.dot(picks, read(side), preferred_element_type=jnp.float32)
            halves.append(found.reshape(step // RANKS, RANKS, len(outs) * HEAD_DIM))
        joined = jnp.concatenate(halves, axis=1).astype(jnp.bfloat16)
        for i, out in enumerate(outs):
            out[pl.ds(part * (step // RANKS), step // RANKS), 0] = joined[
                :, :, i * HEAD_DIM : (i + 1) * HEAD_DIM
            ]
        return carry

    lax.fori_loop(0, CLUSTERS * RANKS // step, body, 0)


def dispatch_kernel(count, slot_ref, *refs):
    sources, outs = refs[:count], refs[count:]
    rows = slot_ref.shape[-1]

    def read(side):
        return jnp.concatenate([s[side].reshape(rows, HEAD_DIM) for s in sources], axis=1)

    dispatch_rows(slot_ref, read, outs)


def slot_block(index):
    return pl.BlockSpec((CLUSTERS, 1, 2 * RANKS, HEAD_DIM), index)


def dispatch(slots, arrays, name):
    devices, rows = slots.shape
    pairs = devices // 2
    in_specs = [pl.BlockSpec((1, 2, rows), lambda i: (i, 0, 0))]
    operands = [slots.reshape(pairs, 2, rows)]
    for array, part in arrays:
        if part is None:
            in_specs.append(pl.BlockSpec((2, rows, HEAD_DIM), lambda i: (i, 0, 0)))
        else:
            in_specs.append(
                pl.BlockSpec((2, 1, rows, HEAD_DIM), lambda i, part=part: (i, part, 0, 0))
            )
        operands.append(array)
    count = len(arrays)
    shape = (CLUSTERS, pairs, 2 * RANKS, HEAD_DIM)
    flops = 2 * devices * rows * CLUSTERS * RANKS * HEAD_DIM * count
    return pl.pallas_call(
        functools.partial(dispatch_kernel, count),
        grid=(pairs,),
        in_specs=in_specs,
        out_specs=[slot_block(lambda i: (0, i, 0, 0))] * count,
        out_shape=[jax.ShapeDtypeStruct(shape, jnp.bfloat16)] * count,
        compiler_params=params(),
        cost_estimate=pl.CostEstimate(
            flops=flops, bytes_accessed=12_000_000 * count, transcendentals=0
        ),
        name=name,
    )(*operands)


def attend_clusters(own, bias_ref, own_k, own_v, pair_k, pair_v, query, mixed, start):
    block, pairs, lines, width = own_k.shape
    slots = pairs * lines
    batch = 32
    lane = iota((slots, 2 * slots), 1)
    row = iota((slots, 2 * slots), 0)
    causal = jnp.where((lane <= row) | (lane >= slots), 0.0, NEGATIVE)
    lane = iota((1, 128), 1)
    ones = jnp.ones((4 * slots, 128), jnp.bfloat16)
    none = jnp.zeros((slots, 2 * slots), jnp.bfloat16)

    def read(ref, c):
        return ref[c].reshape(slots, width)

    def body(step, carry):
        base = step * batch
        pieces = []
        for j in range(0, batch, 2):
            here = (base + j, base + j + 1)
            keys = [read(ref, c) for c in here for ref in (own_k, pair_k)]
            asked = [read(query, c) for c in here]
            scores = contract_last(jnp.concatenate(asked, axis=0), jnp.concatenate(keys, axis=0))
            for i, c in enumerate(here):
                part = scores[i * slots : (i + 1) * slots, i * 2 * slots : (i + 1) * 2 * slots]
                part = part + bias_ref[pl.ds(c, 1), :]
                pieces.append(part + causal if own else part)
        scores = jnp.concatenate(pieces, axis=0)
        peak = jnp.max(scores, axis=1, keepdims=True)
        upper = peak.astype(jnp.bfloat16).astype(jnp.float32)
        lower = (peak - upper).astype(jnp.bfloat16).astype(jnp.float32)
        peak = upper + lower
        weights = jnp.exp2((scores - peak) * SCALE)
        weights = weights.astype(jnp.bfloat16)
        pieces = []
        for j in range(0, batch, 2):
            here = (base + j, base + j + 1)
            values = [read(ref, c) for c in here for ref in (own_v, pair_v)]
            values = jnp.concatenate([jnp.concatenate(values, axis=0), ones], axis=1)
            first = jnp.concatenate([weights[j * slots : (j + 1) * slots], none], axis=1)
            second = jnp.concatenate([none, weights[(j + 1) * slots : (j + 2) * slots]], axis=1)
            pieces.append(
                jnp.dot(
                    jnp.concatenate([first, second], axis=0),
                    values,
                    preferred_element_type=jnp.float32,
                )
            )
        mixture = jnp.concatenate(pieces, axis=0)
        total = mixture[:, width:]
        mixture = mixture[:, :width] * (1.0 / total)
        high = total.astype(jnp.bfloat16).astype(jnp.float32)
        stats = jnp.where(lane == 2, high, total - high)
        stats = jnp.where(lane == 0, upper, jnp.where(lane == 1, lower, stats))
        both = jnp.concatenate([mixture, stats], axis=1).astype(jnp.bfloat16)
        mixed[pl.ds(start + base, batch)] = both.reshape(batch, pairs, lines, 2 * width)
        return carry

    lax.fori_loop(0, block // batch, body, 0)


def collect_rows(index, slot_ref, mixed, outs, held):
    rows = slot_ref.shape[1]
    clusters, _, lines, width = mixed.shape
    step = 256
    eye = iota((128, 128), 0) == iota((128, 128), 1)
    part_rows = rows // HALVES
    chunks = part_rows // 128
    sub = iota((chunks, 128), 0)

    def as_line(column):
        return jnp.sum(jnp.where(eye, column, 0.0), axis=0, keepdims=True)

    for side in range(2):
        wide = mixed[:, pl.ds(index, 1)].reshape(clusters, lines, width).astype(jnp.float32)
        held[...] = (
            wide[:, side * RANKS : (side + 1) * RANKS]
            .reshape(clusters * RANKS, width)
            .astype(jnp.bfloat16)
        )
        for half, out_ref in enumerate(outs):
            peaks = jnp.zeros((chunks, 128), jnp.float32)
            totals = jnp.zeros((chunks, 128), jnp.float32)
            for first in range(0, part_rows, step):
                start = half * part_rows + first
                column = slot_ref[0, start : start + step, side : side + 1]
                picks = as_mask(iota((step, clusters * RANKS), 1) == column)
                found = jnp.dot(picks, held[...], preferred_element_type=jnp.float32)
                out_ref[side, first : first + step] = found[:, :HEAD_DIM].astype(jnp.bfloat16)
                stat = [found[:, HEAD_DIM + i : HEAD_DIM + i + 1] for i in range(4)]
                peak, total = stat[0] + stat[1], stat[2] + stat[3]
                for piece in range(step // 128):
                    here = slice(piece * 128, (piece + 1) * 128)
                    place = sub == first // 128 + piece
                    peaks = jnp.where(place, as_line(peak[here]), peaks)
                    totals = jnp.where(place, as_line(total[here]), totals)
            upper = peaks.astype(jnp.bfloat16).astype(jnp.float32)
            high = totals.astype(jnp.bfloat16).astype(jnp.float32)
            stats = jnp.concatenate([upper, peaks - upper, high, totals - high], axis=0)
            out_ref[side, part_rows : part_rows + STAT_ROWS] = stats.astype(jnp.bfloat16)


def answer_kernel(own, steps, bias_ref, own_k, own_v, pair_k, pair_v, query, slot_ref, *refs):
    *outs, mixed, held = refs
    step = pl.program_id(0)
    block = own_k.shape[0]

    @pl.when(step < steps)
    def _():
        attend_clusters(
            own, bias_ref, own_k, own_v, pair_k, pair_v, query, mixed, step * block
        )

    @pl.when(step >= steps)
    def _():
        collect_rows(step - steps, slot_ref, mixed, outs, held)


def answer(bias, own_k, own_v, pair_k, pair_v, query, slots, own, name):
    clusters, pairs, lines, width = own_k.shape
    devices, rows = slots.shape
    block = 64
    steps = clusters // block
    columns = jnp.transpose(slots.reshape(pairs, 2, rows), (0, 2, 1))
    tall = rows // HALVES + STAT_ROWS
    last = steps - 1
    spec = pl.BlockSpec(
        (block, pairs, lines, width), lambda i: (jnp.minimum(i, last), 0, 0, 0)
    )
    return pl.pallas_call(
        functools.partial(answer_kernel, own, steps),
        grid=(steps + pairs,),
        in_specs=[pl.BlockSpec((block, 2 * pairs * lines), lambda i: (jnp.minimum(i, last), 0))]
        + [spec] * 5
        + [pl.BlockSpec((1, rows, 2), lambda i: (jnp.maximum(i - steps, 0), 0, 0))],
        out_specs=[
            pl.BlockSpec((2, tall, HEAD_DIM), lambda i: (jnp.maximum(i - steps, 0), 0, 0))
        ]
        * HALVES,
        out_shape=[jax.ShapeDtypeStruct((devices, tall, HEAD_DIM), jnp.bfloat16)] * HALVES,
        scratch_shapes=[
            pltpu.VMEM((clusters, pairs, lines, 2 * width), jnp.bfloat16),
            pltpu.VMEM((clusters * RANKS, 2 * width), jnp.bfloat16),
        ],
        compiler_params=params(),
        cost_estimate=pl.CostEstimate(
            flops=2 * devices * rows * clusters * RANKS * 2 * width,
            bytes_accessed=30_000_000,
            transcendentals=0,
        ),
        name=name,
    )(bias, own_k, own_v, pair_k, pair_v, query, columns)


def window_kernel(first_ref, q_ref, own_k, own_v, past_k, past_v, out_ref):
    rows = q_ref.shape[0]
    step = 256
    row = iota((step, step), 0)
    column = iota((step, step), 1)

    def run(with_past):
        for part in range(rows // step):
            query = q_ref[part * step : (part + 1) * step]
            stop = (part + 1) * step
            keys, values = own_k[:stop], own_v[:stop]
            if with_past:
                keys = jnp.concatenate([past_k[part * step :], keys], axis=0)
                values = jnp.concatenate([past_v[part * step :], values], axis=0)
            scores = contract_last(query, keys)
            span = scores.shape[1]
            pieces = []
            if with_past:
                pieces.append(jnp.where(column > row, scores[:, :step], NEGATIVE))
                pieces.append(scores[:, step : span - step])
            elif span > step:
                pieces.append(scores[:, : span - step])
            pieces.append(jnp.where(column <= row, scores[:, span - step :], NEGATIVE))
            scores = jnp.concatenate(pieces, axis=1) if len(pieces) > 1 else pieces[0]
            peak = jnp.max(scores, axis=1, keepdims=True)
            weights = jnp.exp2((scores - peak) * SCALE)
            total = jnp.sum(weights, axis=1, keepdims=True)
            mixture = jnp.dot(
                weights.astype(jnp.bfloat16), values, preferred_element_type=jnp.float32
            )
            out_ref[part * step : (part + 1) * step] = (mixture * (1.0 / total)).astype(
                jnp.bfloat16
            )

    pl.when(first_ref[0] == 0)(lambda: run(False))
    pl.when(first_ref[0] != 0)(lambda: run(True))


def window_heads(my_index, query_rows, key_rows, value_rows, past):
    rows, width = query_rows.shape
    own = pl.BlockSpec((rows, HEAD_DIM), lambda h: (0, h))
    return pl.pallas_call(
        window_kernel,
        grid=(HEADS_L,),
        in_specs=[pl.BlockSpec(memory_space=pltpu.SMEM)] + [own] * 5,
        out_specs=own,
        out_shape=jax.ShapeDtypeStruct((rows, width), jnp.bfloat16),
        compiler_params=params(),
        cost_estimate=pl.CostEstimate(
            flops=8 * HEADS_L * rows * 1280 * HEAD_DIM,
            bytes_accessed=14_000_000,
            transcendentals=0,
        ),
        name="window_heads",
    )(my_index.reshape(1), query_rows, key_rows, value_rows, *past)


def merge_kernel(count, valid_ref, *refs):
    parts, out_ref = refs[:count], refs[count]
    rows = out_ref.shape[0]
    eye = iota((128, 128), 0) == iota((128, 128), 1)
    n = rows // 128
    peaks, totals = [], []
    for i, part in enumerate(parts):
        stats = part[rows : rows + STAT_ROWS].astype(jnp.float32)
        peaks.append(jnp.where(valid_ref[i] != 0, stats[:n] + stats[n : 2 * n], NEGATIVE))
        totals.append(stats[2 * n : 3 * n] + stats[3 * n : 4 * n])
    highest = functools.reduce(jnp.maximum, peaks)
    shares = [t * jnp.exp2((peak - highest) * SCALE) for t, peak in zip(totals, peaks)]
    whole = functools.reduce(jnp.add, shares)
    shares = [share / whole for share in shares]
    for piece in range(n):
        here = slice(piece * 128, (piece + 1) * 128)
        result = jnp.zeros((128, HEAD_DIM), jnp.float32)
        for part, share in zip(parts, shares):
            column = jnp.sum(
                jnp.where(eye, share[piece : piece + 1], 0.0), axis=1, keepdims=True
            )
            result = result + part[here].astype(jnp.float32) * column
        out_ref[here] = result.astype(jnp.bfloat16)


def merge(parts, valid):
    devices, tall, width = parts[0].shape
    rows = tall - STAT_ROWS
    return pl.pallas_call(
        functools.partial(merge_kernel, len(parts)),
        grid=(devices,),
        in_specs=[pl.BlockSpec(memory_space=pltpu.SMEM)]
        + [pl.BlockSpec((None, tall, width), lambda i: (i, 0, 0))] * len(parts),
        out_specs=pl.BlockSpec((None, rows, width), lambda i: (i, 0, 0)),
        out_shape=jax.ShapeDtypeStruct((devices, rows, width), jnp.bfloat16),
        compiler_params=params(),
        name="merge_parts",
    )(valid, *parts)


def place_kernel(base_ref, heads_ref, out_ref):
    del base_ref
    for head in range(HEADS_R):
        out_ref[:, head * HEAD_DIM : (head + 1) * HEAD_DIM] = heads_ref[head]


def place_heads(base, heads, half):
    rows, width = base.shape
    block = 256
    steps = rows // HALVES // block
    return pl.pallas_call(
        place_kernel,
        grid=(steps,),
        in_specs=[
            pl.BlockSpec(memory_space=pl.ANY),
            pl.BlockSpec((HEADS_R, block, HEAD_DIM), lambda i: (0, i, 0)),
        ],
        out_specs=pl.BlockSpec((block, HEADS_R * HEAD_DIM), lambda i: (half * steps + i, 1)),
        out_shape=jax.ShapeDtypeStruct((rows, width), jnp.bfloat16),
        input_output_aliases={0: 0},
        compiler_params=params(),
        name="place_heads",
    )(base, heads)


def heads_kernel(in_ref, out_ref):
    for head in range(HEADS_R):
        out_ref[head] = in_ref[:, head * HEAD_DIM : (head + 1) * HEAD_DIM]


def heads_first(matrix):
    rows = matrix.shape[0]
    block = 256
    return pl.pallas_call(
        heads_kernel,
        grid=(rows // block,),
        in_specs=[pl.BlockSpec((block, HEADS_R * HEAD_DIM), lambda i: (i, 1))],
        out_specs=pl.BlockSpec((HEADS_R, block, HEAD_DIM), lambda i: (0, i, 0)),
        out_shape=jax.ShapeDtypeStruct((HEADS_R, rows, HEAD_DIM), jnp.bfloat16),
        compiler_params=params(),
        name="heads_first",
    )(matrix)


def on_device(query_rows, key_rows, value_rows, cluster_ids):
    rows = query_rows.shape[0]
    local_width = HEADS_L * HEAD_DIM
    device_count = lax.axis_size(AXES)
    my_index = lax.axis_index(AXES)
    group = HEADS_R
    planes = device_count // group
    couples = planes // 2
    plane = my_index // group
    place = my_index % group
    groups = [[group * i + j for j in range(group)] for i in range(planes)]

    def swap(array):
        return lax.all_to_all(
            array, AXES, split_axis=0, concat_axis=0, tiled=True, axis_index_groups=groups
        )

    def move(array, routes):
        pairs = [(group * a + j, group * b + j) for a, b in routes for j in range(group)]
        return lax.ppermute(array, AXES, pairs)

    def after(array, *others):
        return lax.optimization_barrier((array, *others))

    slots, counts = rank_tokens(cluster_ids)
    facts = lax.all_gather(jnp.concatenate([slots, counts], axis=1), AXES)
    facts = lax.dynamic_index_in_dim(facts, place, 1, keepdims=False)
    facts = facts.reshape(planes, group, rows + CLUSTERS)

    def visit_routes(shift, side):
        return [(2 * j + side, 2 * (j - shift) + 1) for j in range(shift, couples)]

    pair_routes = [(2 * j, 2 * j + 1) for j in range(couples)]
    keys = swap(heads_first(key_rows))
    pair_keys = move(keys, pair_routes)
    q_heads, keys = after(heads_first(query_rows), keys)
    queries = swap(q_heads)

    def visit(queries, shift):
        first = move(queries, visit_routes(shift, 0))
        queries, first = after(queries, first)
        return [first, move(queries, visit_routes(shift, 1))]

    visitors = visit(queries, 1) if couples > 1 else []
    v_heads, queries = after(heads_first(value_rows), queries)
    values = swap(v_heads)
    pair_values = move(values, pair_routes)
    past = [key_rows[:, :local_width], value_rows[:, :local_width]]
    *past, pair_values = after(past[0], past[1], pair_values)
    past = [lax.ppermute(m, AXES, [(i, i + 1) for i in range(device_count - 1)]) for m in past]

    def facts_of(index):
        return lax.dynamic_index_in_dim(facts, index, 0, keepdims=False)

    def bias_of(held):
        filled = jnp.arange(RANKS, dtype=jnp.int32)[None, None, :] < held.T[:, :, None]
        return jnp.where(filled, 0.0, NEGATIVE).reshape(CLUSTERS, group * RANKS)

    def visit_slots(shift):
        homes = [2 * (plane // 2 + shift) + side for side in range(2)]
        return [facts_of(jnp.minimum(home, planes - 1))[:, :rows] for home in homes]

    own_facts = facts_of(plane)
    pair_facts = facts_of(plane ^ 1)
    is_odd = plane % 2 == 1
    bias = jnp.concatenate(
        [bias_of(own_facts[:, rows:]), jnp.where(is_odd, bias_of(pair_facts[:, rows:]), NEGATIVE)],
        axis=1,
    )
    own_q, own_k, own_v = dispatch(
        own_facts[:, :rows], [(queries, None), (keys, None), (values, None)], "dispatch_own"
    )
    (pair_k,) = dispatch(pair_facts[:, :rows], [(pair_keys, None)], "dispatch_pair_keys")
    homes = visit_slots(1)
    asked = []
    if couples > 1:
        asked = list(dispatch(homes[0], [(visitors[0], None)], "dispatch_visit"))
        pair_values, pair_k, own_q, asked[0] = after(pair_values, pair_k, own_q, asked[0])
    (pair_v,) = dispatch(pair_facts[:, :rows], [(pair_values, None)], "dispatch_pair_values")
    kept = (bias, own_k, own_v, pair_k, pair_v)

    parts, valid = [], [jnp.int32(1)]
    for shift in range(1, couples):
        homes = visit_slots(shift)
        if shift > 1:
            queries, parts[-1][-1] = after(queries, parts[-1][-1])
            visitors = visit(queries, shift)
            asked = list(dispatch(homes[0], [(visitors[0], None)], "dispatch_visit"))
        for side in range(2):
            if side == 1:
                asked = dispatch(homes[1], [(visitors[1], None)], "dispatch_visit")
            found = list(answer(*kept, asked[0], homes[side], False, "answer_visit"))
            if side == 0:
                visitors[1], found[0] = after(visitors[1], found[0])
            elif shift == 1:
                own_q, found[0] = after(own_q, found[0])
            routes = [(b, a) for a, b in visit_routes(shift, side)]
            back = []
            for half in range(HALVES):
                if half:
                    found[half], back[-1] = after(found[half], back[-1])
                back.append(move(found[half], routes))
            parts.append(back)
            valid.append(((plane // 2 >= shift) & (plane % 2 == side)).astype(jnp.int32))
    own_found = list(answer(*kept, own_q, own_facts[:, :rows], True, "answer_own"))
    past[0], own_found[0] = after(past[0], own_found[0])
    result = window_heads(my_index, query_rows, key_rows, value_rows, past)
    valid = jnp.stack(valid)
    if parts:
        parts[-1][0], result = after(parts[-1][0], result)
    merged = []
    for half in range(HALVES):
        joined = merge([own_found[half]] + [back[half] for back in parts], valid)
        if half:
            joined, merged[-1] = after(joined, merged[-1])
        merged.append(swap(joined))
    for half in range(HALVES):
        result = place_heads(result, merged[half], half)
    return result


def solution(mesh):
    return jax.shard_map(
        on_device,
        mesh=mesh,
        in_specs=(P(AXES, None), P(AXES, None), P(AXES, None), P(None, AXES)),
        out_specs=P(AXES, None),
        check_vma=False,
    )
```

time: 501 us -> 359 us (0.72)
  the two profiles are of different devices: /device:TPU:16 before, /device:TPU:24 now
where the time goes in v2:
time: 359 us; the launch traced here: 358 us
  Pallas kernels  199 us (55%)
  waiting for transfers between devices  79.3 us (22%)
  starting transfers between devices  47.7 us (13%)
  local copies, waits for them, and re-layouts  15.5 us (4%)
  between operations  13.7 us (4%)
    pallas_call x5, Pallas kernels, dispatch(): pl.pallas_call(functools.partial(dispatch_kernel, count), grid=(pairs,),...  70.8 us
    pallas_call x3, Pallas kernels, answer(): pl.pallas_call(functools.partial(answer_kernel, own, steps), grid=(steps...  69.3 us
    all_to_all x5, waiting for transfers between devices, swap(): lax.all_to_all(array, AXES, split_axis=0, concat_axis=0, tiled=True, axis...  61.6 us
    ppermute x8, starting transfers between devices, move(): return lax.ppermute(array, AXES, pairs)  22.3 us
    pallas_call x1, Pallas kernels, window_heads(): pl.pallas_call(window_kernel, grid=(HEADS_L,), in_specs=[pl.BlockSpec(mem...  21.7 us
    all_to_all x5, starting transfers between devices, swap(): lax.all_to_all(array, AXES, split_axis=0, concat_axis=0, tiled=True, axis...  19.6 us
    ppermute x8, waiting for transfers between devices, move(): return lax.ppermute(array, AXES, pairs)  17.8 us
    pallas_call x2, Pallas kernels, merge(): pl.pallas_call(functools.partial(merge_kernel, len(parts)), grid=(devices...  13.8 us
  transfers between devices with their start and end apart: 16, of which 6 were waited for; matrix products, arithmetic and copies ran while one was open for 5% of the time, Pallas kernels for 54%

profile of v2, /device:TPU:24, one launch (start us, length us, event | category | flops | bytes accessed | tf_op | source)
XLA Modules:
  0.0 357.6 jit_solution(518977732231835299)
XLA Ops:
  6.5 3.9 %heads_first.5 = bf16[8,1024,128]{2,1,0:T(8,128)(2,1)} custom-call(bf16[1024,2048]{1,0:T(8,128)(2,1)} %own_k.1), custom_call_target="tpu_custom_call" | custom-call | tf_op jit(solution)/shard_map/heads_first/pallas_call | solution.py:436
  10.5 3.7 %all-to-all-start = ((bf16[8,1024,128]{2,1,0:T(8,128)(2,1)}), bf16[8,1024,128]{2,1,0:T(8,128)(2,1)S(1)}, u32[]{:S(2)}, u32[]{:S(2)}) async-start(bf16[8,1024,128]{2,1,0:T(8,128)(2,1)} %heads_first.5), calls=%async_computation | async-start | bytes 4194304 | tf_op jit(solution)/shard_map/all_to_all | solution.py:460
  14.2 0.0 all-gather.3.cloned.1.call-start
  14.2 6.9 %rank_tokens.1 = (s32[8,1024]{1,0:T(8,128)}, s32[8,256]{1,0:T(8,128)}) custom-call(s32[8,1024]{1,0:T(8,128)} %ids_ref.1), custom_call_target="tpu_custom_call" | custom-call | tf_op jit(solution)/shard_map/rank_tokens/pallas_call | solution.py:56
  21.1 1.4 pad_add_fusion
  22.5 0.0 all-gather.3.cloned.1.call-update
  22.6 3.9 %heads_first.4 = bf16[8,1024,128]{2,1,0:T(8,128)(2,1)} custom-call(bf16[1024,2048]{1,0:T(8,128)(2,1)} %q_ref.1), custom_call_target="tpu_custom_call" | custom-call | tf_op jit(solution)/shard_map/heads_first/pallas_call | solution.py:436
  26.5 13.7 %all-to-all-done.refs_1_ = bf16[8,1024,128]{2,1,0:T(8,128)(2,1)S(1)} async-done(((bf16[8,1024,128]{2,1,0:T(8,128)(2,1)}), bf16[8,1024,128]{2,1,0:T(8,128)(2,1)S(1)}, u32[]{:S(2)}, u32[]{:S(2)}) %all-to-all-start) | async-done | bytes 2097184 | tf_op jit(solution)/shard_map/all_to_all | solution.py:460
  40.2 4.4 %all-to-all-start.1 = ((bf16[8,1024,128]{2,1,0:T(8,128)(2,1)}), bf16[8,1024,128]{2,1,0:T(8,128)(2,1)}, u32[]{:S(2)}, u32[]{:S(2)}) async-start(bf16[8,1024,128]{2,1,0:T(8,128)(2,1)} %heads_first.4), calls=%async_computation.1 | async-start | bytes 4194304 | tf_op jit(solution)/shard_map/all_to_all | solution.py:460
  44.6 1.3 collective-permute-start.1
  45.9 3.9 %heads_first.3 = bf16[8,1024,128]{2,1,0:T(8,128)(2,1)} custom-call(bf16[1024,2048]{1,0:T(8,128)(2,1)} %own_v.1), custom_call_target="tpu_custom_call" | custom-call | tf_op jit(solution)/shard_map/heads_first/pallas_call | solution.py:436
  49.8 23.9 %all-to-all-done.1.refs_0_ = bf16[8,1024,128]{2,1,0:T(8,128)(2,1)} async-done(((bf16[8,1024,128]{2,1,0:T(8,128)(2,1)}), bf16[8,1024,128]{2,1,0:T(8,128)(2,1)}, u32[]{:S(2)}, u32[]{:S(2)}) %all-to-all-start.1) | async-done | bytes 2097184 | tf_op jit(solution)/shard_map/all_to_all | solution.py:460
  73.7 4.4 %all-to-all-start.2 = ((bf16[8,1024,128]{2,1,0:T(8,128)(2,1)}), bf16[8,1024,128]{2,1,0:T(8,128)(2,1)}, u32[]{:S(2)}, u32[]{:S(2)}) async-start(bf16[8,1024,128]{2,1,0:T(8,128)(2,1)} %heads_first.3), calls=%async_computation.2 | async-start | bytes 4194304 | tf_op jit(solution)/shard_map/all_to_all | solution.py:460
  78.1 2.0 collective-permute-start.2
  80.1 3.3 slice.30
  83.4 1.5 slice.31
  84.9 0.1 lt.73
  85.0 1.4 constant_dynamic-slice_fusion
  86.5 0.6 reshape.32.slot_ref
  87.2 0.6 reshape.33.slot_ref
  87.8 2.0 copy.14
  89.8 0.1 copy.12
  89.9 0.1 copy.13
  90.1 2.0 copy.15
  92.1 11.7 %all-to-all-done.2.refs_2_ = bf16[8,1024,128]{2,1,0:T(8,128)(2,1)} async-done(((bf16[8,1024,128]{2,1,0:T(8,128)(2,1)}), bf16[8,1024,128]{2,1,0:T(8,128)(2,1)}, u32[]{:S(2)}, u32[]{:S(2)}) %all-to-all-start.2) | async-done | bytes 2097184 | tf_op jit(solution)/shard_map/all_to_all | solution.py:460
  103.8 1.3 collective-permute-start
  105.1 0.8 pad_maximum_fusion.bias_ref
  105.8 0.0 collective-permute-done.1.refs_0_
  105.8 12.2 %dispatch_pair_keys.1.pair_k = bf16[256,4,16,128]{3,2,1,0:T(8,128)(2,1)} custom-call(s32[4,2,1024]{2,1,0:T(2,128)} %reshape.33.slot_ref, bf16[8,1024,128]{2,1,0:T(8,128)(2,1)} %collective-permute-done.1.refs_0_), custom_call_target="tpu_custom_call" | custom-call | flops 4294967296 | bytes 12000000 | tf_op jit(solution)/shard_map/dispatch_pair_keys/pallas_call | solution.py:139
  118.0 0.0 collective-permute-done.2.refs_0_
  118.0 12.5 %collective-permute-start.3 = (bf16[8,1024,128]{2,1,0:T(8,128)(2,1)}, bf16[8,1024,128]{2,1,0:T(8,128)(2,1)S(1)}, u32[]{:S(2)}, u32[]{:S(2)}) collective-permute-start(bf16[8,1024,128]{2,1,0:T(8,128)(2,1)} %all-to-all-done.1.refs_0_), channel_id=1, source_target_pairs={{24,8},{25,9},{26,10},{27,11},{28,12},{29,13},{30,14},{31,15}} | collective-permute-start | bytes 6291464 | tf_op jit(solution)/shard_map/ppermute | solution.py:466
  130.5 21.9 %dispatch_own.1 = (bf16[256,4,16,128]{3,2,1,0:T(8,128)(2,1)}, bf16[256,4,16,128]{3,2,1,0:T(8,128)(2,1)}, bf16[256,4,16,128]{3,2,1,0:T(8,128)(2,1)}) custom-call(s32[4,2,1024]{2,1,0:T(2,128)} %reshape.32.slot_ref, bf16[8,1024,128]{2,1,0:T(8,128)(2,1)} %all-to-all-done.1.refs_0_, bf16[8,1024,128]{2,1,0:T(8,128)(2,1)} %copy-done.3, ...), custom_call_target="tpu_custom_call" | custom-call | flops 12884901888 | bytes 36000000 | tf_op jit(solution)/shard_map/dispatch_own/pallas_call | solution.py:139
  152.5 12.3 %dispatch_visit.2.query = bf16[256,4,16,128]{3,2,1,0:T(8,128)(2,1)} custom-call(s32[4,2,1024]{2,1,0:T(2,128)} %copy-done.8, bf16[8,1024,128]{2,1,0:T(8,128)(2,1)} %collective-permute-done.2.refs_0_), custom_call_target="tpu_custom_call" | custom-call | flops 4294967296 | bytes 12000000 | tf_op jit(solution)/shard_map/dispatch_visit/pallas_call | solution.py:139
  164.8 0.0 collective-permute-done.refs_0_
  164.8 1.9 collective-permute-start.5
  166.8 3.9 %collective-permute-start.6 = (bf16[1024,1024]{1,0:T(8,128)(2,1)S(1)}, bf16[1024,1024]{1,0:T(8,128)(2,1)}, u32[]{:S(2)}, u32[]{:S(2)}) collective-permute-start(bf16[1024,1024]{1,0:T(8,128)(2,1)S(1)} %copy-done.4), channel_id=1, source_target_pairs={{0,1},{1,2},{2,3},{3,4},{4,5},{5,6},{6,7},{7,8},{8,9},{9,10},{10,1... | collective-permute-start | bytes 6291464 | tf_op jit(solution)/shard_map/ppermute | solution.py:496
  170.7 12.2 %dispatch_pair_values.1.pair_v = bf16[256,4,16,128]{3,2,1,0:T(8,128)(2,1)} custom-call(s32[4,2,1024]{2,1,0:T(2,128)} %reshape.33.slot_ref, bf16[8,1024,128]{2,1,0:T(8,128)(2,1)} %copy-done.10), custom_call_target="tpu_custom_call" | custom-call | flops 4294967296 | bytes 12000000 | tf_op jit(solution)/shard_map/dispatch_pair_values/pallas_call | solution.py:139
  182.9 23.1 %answer_visit.2 = (bf16[8,528,128]{2,1,0:T(8,128)(2,1)}, bf16[8,528,128]{2,1,0:T(8,128)(2,1)}) custom-call(f32[256,128]{1,0:T(8,128)} %pad_maximum_fusion.bias_ref, bf16[256,4,16,128]{3,2,1,0:T(8,128)(2,1)} %get-tuple-element.49.own_k, bf16[256,4,16,128]{3,2,1,0:T(8,128)(2,1)} %get-tuple-element.50.own_v, ...), custom_call_target="tpu_custom_call" | custom-call | flops 8589934592 | bytes 30000000 | tf_op jit(solution)/shard_map/answer_visit/pallas_call | solution.py:281
  206.0 0.0 collective-permute-done.3.refs_0_
  206.0 0.7 collective-permute-start.7
  206.7 0.6 copy-done.9
  207.3 12.2 %dispatch_visit.3.query = bf16[256,4,16,128]{3,2,1,0:T(8,128)(2,1)} custom-call(s32[4,2,1024]{2,1,0:T(2,128)} %copy-done.7, bf16[8,1024,128]{2,1,0:T(8,128)(2,1)} %copy-done.9), custom_call_target="tpu_custom_call" | custom-call | flops 4294967296 | bytes 12000000 | tf_op jit(solution)/shard_map/dispatch_visit/pallas_call | solution.py:139
  219.5 23.0 %answer_visit.3 = (bf16[8,528,128]{2,1,0:T(8,128)(2,1)}, bf16[8,528,128]{2,1,0:T(8,128)(2,1)}) custom-call(f32[256,128]{1,0:T(8,128)} %pad_maximum_fusion.bias_ref, bf16[256,4,16,128]{3,2,1,0:T(8,128)(2,1)} %get-tuple-element.49.own_k, bf16[256,4,16,128]{3,2,1,0:T(8,128)(2,1)} %get-tuple-element.50.own_v, ...), custom_call_target="tpu_custom_call" | custom-call | flops 8589934592 | bytes 30000000 | tf_op jit(solution)/shard_map/answer_visit/pallas_call | solution.py:281
  242.5 1.5 collective-permute-start.4
  244.1 0.6 add_convert_fusion.valid_ref
  244.6 2.0 copy.16
  246.6 23.2 %answer_own.1 = (bf16[8,528,128]{2,1,0:T(8,128)(2,1)}, bf16[8,528,128]{2,1,0:T(8,128)(2,1)}) custom-call(f32[256,128]{1,0:T(8,128)} %pad_maximum_fusion.bias_ref, bf16[256,4,16,128]{3,2,1,0:T(8,128)(2,1)} %get-tuple-element.49.own_k, bf16[256,4,16,128]{3,2,1,0:T(8,128)(2,1)} %get-tuple-element.50.own_v, bf16[256,4,16,128]{3,2,1,0:T(8,128)(2,1)} %dispatch_pair_keys.1.pair_k, ...), custom_call_target="tpu_custom_call" | custom-call | flops 8589934592 | bytes 30000000 | tf_op jit(solution)/shard_map/answer_own/pallas_call | solution.py:281
  269.9 0.0 collective-permute-done.7.refs_1_
  269.9 1.5 collective-permute-done.4.refs_2_
  271.4 1.6 collective-permute-start.8
  273.1 1.3 collective-permute-start.9
  274.4 0.0 collective-permute-done.5.past_k
  274.4 0.0 collective-permute-done.6.past_v
  274.4 21.7 %window_heads.1.base_ref = bf16[1024,2048]{1,0:T(8,128)(2,1)} custom-call(s32[1]{0:T(128)} %bitcast.11.first_ref, bf16[1024,2048]{1,0:T(8,128)(2,1)} %q_ref.1, bf16[1024,2048]{1,0:T(8,128)(2,1)} %own_k.1, bf16[1024,2048]{1,0:T(8,128)(2,1)} %own_v.1, bf16[1024,1024]{1,0:T(8,128)(2,1)} %collective-permute-done.5.past_k, ...), custom_call_target="tpu_custom_call" | custom-call | flops 10737418240 | bytes 14000000 | tf_op jit(solution)/shard_map/window_heads/pallas_call | solution.py:347
  296.1 6.9 %merge_parts.3 = bf16[8,512,128]{2,1,0:T(8,128)(2,1)} custom-call(s32[3]{0:T(128)} %add_convert_fusion.valid_ref, bf16[8,528,128]{2,1,0:T(8,128)(2,1)} %get-tuple-element.76.refs_0_, bf16[8,528,128]{2,1,0:T(8,128)(2,1)} %copy-done.5, bf16[8,528,128]{2,1,0:T(8,128)(2,1)} %collective-permute-done.4.refs_2_), custom_call_target="tpu_custom_call" | custom-call | tf_op jit(solution)/shard_map/merge_parts/pallas_call | solution.py:391
  303.0 3.6 all-to-all-start.3
  306.5 16.2 %collective-permute-done.9.refs_2_ = bf16[8,528,128]{2,1,0:T(8,128)(2,1)} collective-permute-done((bf16[8,528,128]{2,1,0:T(8,128)(2,1)}, bf16[8,528,128]{2,1,0:T(8,128)(2,1)}, u32[]{:S(2)}, u32[]{:S(2)}) %collective-permute-start.9) | collective-permute-done | bytes 1081376 | tf_op jit(solution)/shard_map/ppermute | solution.py:466
  322.7 6.9 %merge_parts.2 = bf16[8,512,128]{2,1,0:T(8,128)(2,1)} custom-call(s32[3]{0:T(128)} %add_convert_fusion.valid_ref, bf16[8,528,128]{2,1,0:T(8,128)(2,1)} %get-tuple-element.71.refs_0_, bf16[8,528,128]{2,1,0:T(8,128)(2,1)} %collective-permute-done.8.refs_1_, bf16[8,528,128]{2,1,0:T(8,128)(2,1)} %collective-permute-done.9.refs_2_), custom_call_target="tpu_custom_call" | custom-call | tf_op jit(solution)/shard_map/merge_parts/pallas_call | solution.py:391
  329.6 0.0 all-to-all-done.3.heads_ref
  329.6 3.6 all-to-all-start.4
  333.2 2.2 place_heads.2.base_ref
  335.4 12.2 %all-to-all-done.4.heads_ref = bf16[8,512,128]{2,1,0:T(8,128)(2,1)S(1)} async-done(((bf16[8,512,128]{2,1,0:T(8,128)(2,1)}), bf16[8,512,128]{2,1,0:T(8,128)(2,1)S(1)}, u32[]{:S(2)}, u32[]{:S(2)}) %all-to-all-start.4) | async-done | bytes 1048608 | tf_op jit(solution)/shard_map/all_to_all | solution.py:460
  347.6 1.0 copy-done.2
  348.6 2.2 place_heads.3
  (35 shorter events, 0.2 us)
Async XLA Ops:
  10.5 29.7 %all-to-all-start = ((bf16[8,1024,128]{2,1,0:T(8,128)(2,1)}), bf16[8,1024,128]{2,1,0:T(8,128)(2,1)S(1)}, u32[]{:S(2)}, u32[]{:S(2)}) async-start(bf16[8,1024,128]{2,1,0:T(8,128)(2,1)} %heads_first.5), calls=%async_computation | async-start | bytes 4194304 | tf_op jit(solution)/shard_map/all_to_all | solution.py:460
  14.2 70.8 %all-gather.3.cloned.1.call-start = ((), (), s32[]{:S(2)}) async-start(), calls=%async_computation.5 | async-start | bytes 1351680 | tf_op jit(solution)/shard_map/all_gather | solution.py:472
  40.2 9.6 %copy-start.3 = (bf16[8,1024,128]{2,1,0:T(8,128)(2,1)}, bf16[8,1024,128]{2,1,0:T(8,128)(2,1)S(1)}, u32[]{:S(2)}) copy-start(bf16[8,1024,128]{2,1,0:T(8,128)(2,1)S(1)} %all-to-all-done.refs_1_) | copy-start | bytes 6291460
  40.2 33.5 %all-to-all-start.1 = ((bf16[8,1024,128]{2,1,0:T(8,128)(2,1)}), bf16[8,1024,128]{2,1,0:T(8,128)(2,1)}, u32[]{:S(2)}, u32[]{:S(2)}) async-start(bf16[8,1024,128]{2,1,0:T(8,128)(2,1)} %heads_first.4), calls=%async_computation.1 | async-start | bytes 4194304 | tf_op jit(solution)/shard_map/all_to_all | solution.py:460
  44.6 61.2 %collective-permute-start.1 = (bf16[8,1024,128]{2,1,0:T(8,128)(2,1)S(1)}, bf16[8,1024,128]{2,1,0:T(8,128)(2,1)}, u32[]{:S(2)}, u32[]{:S(2)}) collective-permute-start(bf16[8,1024,128]{2,1,0:T(8,128)(2,1)S(1)} %all-to-all-done.refs_1_), channel_id=1, source_target_pairs={{0,8},{1,9},{2,10},{3,11},{4,12},{5,13},{6,14},{7,15},{16,24},{17,... | collective-permute-start | bytes 6291464 | tf_op jit(solution)/shard_map/ppermute | solution.py:466
  73.7 30.1 %all-to-all-start.2 = ((bf16[8,1024,128]{2,1,0:T(8,128)(2,1)}), bf16[8,1024,128]{2,1,0:T(8,128)(2,1)}, u32[]{:S(2)}, u32[]{:S(2)}) async-start(bf16[8,1024,128]{2,1,0:T(8,128)(2,1)} %heads_first.3), calls=%async_computation.2 | async-start | bytes 4194304 | tf_op jit(solution)/shard_map/all_to_all | solution.py:460
  78.1 39.9 %collective-permute-start.2 = (bf16[8,1024,128]{2,1,0:T(8,128)(2,1)}, bf16[8,1024,128]{2,1,0:T(8,128)(2,1)}, u32[]{:S(2)}, u32[]{:S(2)}) collective-permute-start(bf16[8,1024,128]{2,1,0:T(8,128)(2,1)} %all-to-all-done.1.refs_0_), channel_id=1, source_target_pairs={{16,8},{17,9},{18,10},{19,11},{20,12},{21,13},{22,14},{23,15}} | collective-permute-start | bytes 6291464 | tf_op jit(solution)/shard_map/ppermute | solution.py:466
  80.1 3.3 copy-start
  87.1 4.9 %copy-start.8 = (s32[4,2,1024]{2,1,0:T(2,128)}, s32[4,2,1024]{2,1,0:T(2,128)S(1)}, u32[]{:S(2)}) copy-start(s32[4,2,1024]{2,1,0:T(2,128)S(1)} %reshape.34.slot_ref) | copy-start | bytes 98308
  90.0 27.9 %copy-start.7 = (s32[4,2,1024]{2,1,0:T(2,128)}, s32[4,2,1024]{2,1,0:T(2,128)S(1)}, u32[]{:S(2)}) copy-start(s32[4,2,1024]{2,1,0:T(2,128)S(1)} %reshape.35.slot_ref) | copy-start | bytes 98308
  103.8 61.1 %collective-permute-start = (bf16[8,1024,128]{2,1,0:T(8,128)(2,1)}, bf16[8,1024,128]{2,1,0:T(8,128)(2,1)S(1)}, u32[]{:S(2)}, u32[]{:S(2)}) collective-permute-start(bf16[8,1024,128]{2,1,0:T(8,128)(2,1)} %all-to-all-done.2.refs_2_), channel_id=1, source_target_pairs={{0,8},{1,9},{2,10},{3,11},{4,12},{5,13},{6,14},{7,15},{16,24},{17,... | collective-permute-start | bytes 6291464 | tf_op jit(solution)/shard_map/ppermute | solution.py:466
  118.0 88.0 %collective-permute-start.3 = (bf16[8,1024,128]{2,1,0:T(8,128)(2,1)}, bf16[8,1024,128]{2,1,0:T(8,128)(2,1)S(1)}, u32[]{:S(2)}, u32[]{:S(2)}) collective-permute-start(bf16[8,1024,128]{2,1,0:T(8,128)(2,1)} %all-to-all-done.1.refs_0_), channel_id=1, source_target_pairs={{24,8},{25,9},{26,10},{27,11},{28,12},{29,13},{30,14},{31,15}} | collective-permute-start | bytes 6291464 | tf_op jit(solution)/shard_map/ppermute | solution.py:466
  152.5 14.3 %copy-start.4 = (bf16[1024,1024]{1,0:T(8,128)(2,1)S(1)}, bf16[1024,1024]{1,0:T(8,128)(2,1)}, u32[]{:S(2)}) copy-start(bf16[1024,1024]{1,0:T(8,128)(2,1)} %slice.31) | copy-start | bytes 6291460
  164.8 5.8 %copy-start.10 = (bf16[8,1024,128]{2,1,0:T(8,128)(2,1)}, bf16[8,1024,128]{2,1,0:T(8,128)(2,1)S(1)}, u32[]{:S(2)}) copy-start(bf16[8,1024,128]{2,1,0:T(8,128)(2,1)S(1)} %collective-permute-done.refs_0_) | copy-start | bytes 6291460
  164.8 109.5 %collective-permute-start.5 = (bf16[1024,1024]{1,0:T(8,128)(2,1)}, bf16[1024,1024]{1,0:T(8,128)(2,1)}, u32[]{:S(2)}, u32[]{:S(2)}) collective-permute-start(bf16[1024,1024]{1,0:T(8,128)(2,1)} %slice.30), channel_id=1, source_target_pairs={{0,1},{1,2},{2,3},{3,4},{4,5},{5,6},{6,7},{7,8},{8,9},{9,10},{10,1... | collective-permute-start | bytes 6291464 | tf_op jit(solution)/shard_map/ppermute | solution.py:496
  166.8 107.6 %collective-permute-start.6 = (bf16[1024,1024]{1,0:T(8,128)(2,1)S(1)}, bf16[1024,1024]{1,0:T(8,128)(2,1)}, u32[]{:S(2)}, u32[]{:S(2)}) collective-permute-start(bf16[1024,1024]{1,0:T(8,128)(2,1)S(1)} %copy-done.4), channel_id=1, source_target_pairs={{0,1},{1,2},{2,3},{3,4},{4,5},{5,6},{6,7},{7,8},{8,9},{9,10},{10,1... | collective-permute-start | bytes 6291464 | tf_op jit(solution)/shard_map/ppermute | solution.py:496
  206.0 1.4 copy-start.9
  206.0 63.9 %collective-permute-start.7 = (bf16[8,528,128]{2,1,0:T(8,128)(2,1)}, bf16[8,528,128]{2,1,0:T(8,128)(2,1)S(1)}, u32[]{:S(2)}, u32[]{:S(2)}) collective-permute-start(bf16[8,528,128]{2,1,0:T(8,128)(2,1)} %get-tuple-element.73), channel_id=1, source_target_pairs={{8,16},{9,17},{10,18},{11,19},{12,20},{13,21},{14,22},{15,23}} | collective-permute-start | bytes 3244040 | tf_op jit(solution)/shard_map/ppermute | solution.py:466
  219.5 25.1 %copy-start.6 = (s32[4,2,1024]{2,1,0:T(2,128)S(1)}, s32[4,2,1024]{2,1,0:T(2,128)}, u32[]{:S(2)}) copy-start(s32[4,2,1024]{2,1,0:T(2,128)} %reshape.32.slot_ref) | copy-start | bytes 98308
  242.5 28.9 %collective-permute-start.4 = (bf16[8,528,128]{2,1,0:T(8,128)(2,1)}, bf16[8,528,128]{2,1,0:T(8,128)(2,1)}, u32[]{:S(2)}, u32[]{:S(2)}) collective-permute-start(bf16[8,528,128]{2,1,0:T(8,128)(2,1)} %get-tuple-element.63), channel_id=1, source_target_pairs={{8,24},{9,25},{10,26},{11,27},{12,28},{13,29},{14,30},{15,31}} | collective-permute-start | bytes 3244040 | tf_op jit(solution)/shard_map/ppermute | solution.py:466
  269.9 26.2 %copy-start.5 = (bf16[8,528,128]{2,1,0:T(8,128)(2,1)}, bf16[8,528,128]{2,1,0:T(8,128)(2,1)S(1)}, u32[]{:S(2)}) copy-start(bf16[8,528,128]{2,1,0:T(8,128)(2,1)S(1)} %collective-permute-done.7.refs_1_) | copy-start | bytes 3244036
  271.4 35.1 %collective-permute-start.8 = (bf16[8,528,128]{2,1,0:T(8,128)(2,1)}, bf16[8,528,128]{2,1,0:T(8,128)(2,1)}, u32[]{:S(2)}, u32[]{:S(2)}) collective-permute-start(bf16[8,528,128]{2,1,0:T(8,128)(2,1)} %get-tuple-element.74), channel_id=1, source_target_pairs={{8,16},{9,17},{10,18},{11,19},{12,20},{13,21},{14,22},{15,23}} | collective-permute-start | bytes 3244040 | tf_op jit(solution)/shard_map/ppermute | solution.py:466
  273.1 49.7 %collective-permute-start.9 = (bf16[8,528,128]{2,1,0:T(8,128)(2,1)}, bf16[8,528,128]{2,1,0:T(8,128)(2,1)}, u32[]{:S(2)}, u32[]{:S(2)}) collective-permute-start(bf16[8,528,128]{2,1,0:T(8,128)(2,1)} %get-tuple-element.75), channel_id=1, source_target_pairs={{8,24},{9,25},{10,26},{11,27},{12,28},{13,29},{14,30},{15,31}} | collective-permute-start | bytes 3244040 | tf_op jit(solution)/shard_map/ppermute | solution.py:466
  303.0 26.7 %all-to-all-start.3 = ((bf16[8,512,128]{2,1,0:T(8,128)(2,1)}), bf16[8,512,128]{2,1,0:T(8,128)(2,1)S(1)}, u32[]{:S(2)}, u32[]{:S(2)}) async-start(bf16[8,512,128]{2,1,0:T(8,128)(2,1)} %merge_parts.3), calls=%async_computation.3 | async-start | bytes 2097152 | tf_op jit(solution)/shard_map/all_to_all | solution.py:460
  329.6 3.6 %copy-start.1 = (bf16[8,512,128]{2,1,0:T(8,128)(2,1)}, bf16[8,512,128]{2,1,0:T(8,128)(2,1)S(1)}, u32[]{:S(2)}) copy-start(bf16[8,512,128]{2,1,0:T(8,128)(2,1)S(1)} %all-to-all-done.3.heads_ref) | copy-start | bytes 3145732
  329.6 18.0 %all-to-all-start.4 = ((bf16[8,512,128]{2,1,0:T(8,128)(2,1)}), bf16[8,512,128]{2,1,0:T(8,128)(2,1)S(1)}, u32[]{:S(2)}, u32[]{:S(2)}) async-start(bf16[8,512,128]{2,1,0:T(8,128)(2,1)} %merge_parts.2), calls=%async_computation.4 | async-start | bytes 2097152 | tf_op jit(solution)/shard_map/all_to_all | solution.py:460
  347.6 1.0 copy-start.2
Sparse Core Ops, SparseCore 0:
  22.7 57.4 all-gather.2

commit v3 on v2

--- a/solution.py
+++ b/solution.py
@@ -211,7 +211,7 @@
 
 
 def collect_rows(index, slot_ref, mixed, outs, held):
-    rows = slot_ref.shape[1]
+    rows = slot_ref.shape[-1]
     clusters, _, lines, width = mixed.shape
     step = 256
     eye = iota((128, 128), 0) == iota((128, 128), 1)
@@ -221,6 +221,10 @@
 
     def as_line(column):
         return jnp.sum(jnp.where(eye, column, 0.0), axis=0, keepdims=True)
+
+    def as_column(line):
+        line = line.astype(jnp.float32)
+        return jnp.sum(jnp.where(eye, line, 0.0), axis=1, keepdims=True).astype(jnp.int32)
 
     for side in range(2):
         wide = mixed[:, pl.ds(index, 1)].reshape(clusters, lines, width).astype(jnp.float32)
@@ -234,7 +238,13 @@
             totals = jnp.zeros((chunks, 128), jnp.float32)
             for first in range(0, part_rows, step):
                 start = half * part_rows + first
-                column = slot_ref[0, start : start + step, side : side + 1]
+                column = jnp.concatenate(
+                    [
+                        as_column(slot_ref[0, side : side + 1, i : i + 128])
+                        for i in range(start, start + step, 128)
+                    ],
+                    axis=0,
+                )
                 picks = as_mask(iota((step, clusters * RANKS), 1) == column)
                 found = jnp.dot(picks, held[...], preferred_element_type=jnp.float32)
                 out_ref[side, first : first + step] = found[:, :HEAD_DIM].astype(jnp.bfloat16)
@@ -272,7 +282,6 @@
     devices, rows = slots.shape
     block = 64
     steps = clusters // block
-    columns = jnp.transpose(slots.reshape(pairs, 2, rows), (0, 2, 1))
     tall = rows // HALVES + STAT_ROWS
     last = steps - 1
     spec = pl.BlockSpec(
@@ -283,7 +292,7 @@
         grid=(steps + pairs,),
         in_specs=[pl.BlockSpec((block, 2 * pairs * lines), lambda i: (jnp.minimum(i, last), 0))]
         + [spec] * 5
-        + [pl.BlockSpec((1, rows, 2), lambda i: (jnp.maximum(i - steps, 0), 0, 0))],
+        + [pl.BlockSpec((1, 2, rows), lambda i: (jnp.maximum(i - steps, 0), 0, 0))],
         out_specs=[
             pl.BlockSpec((2, tall, HEAD_DIM), lambda i: (jnp.maximum(i - steps, 0), 0, 0))
         ]
@@ -300,7 +309,7 @@
             transcendentals=0,
         ),
         name=name,
-    )(bias, own_k, own_v, pair_k, pair_v, query, columns)
+    )(bias, own_k, own_v, pair_k, pair_v, query, slots.reshape(pairs, 2, rows))
 
 
 def window_kernel(first_ref, q_ref, own_k, own_v, past_k, past_v, out_ref):
@@ -362,6 +371,11 @@
 
 def merge_kernel(count, valid_ref, *refs):
     parts, out_ref = refs[:count], refs[count]
+    for device in range(out_ref.shape[0]):
+        merge_rows([part.at[device] for part in parts], valid_ref, out_ref.at[device])
+
+
+def merge_rows(parts, valid_ref, out_ref):
     rows = out_ref.shape[0]
     eye = iota((128, 128), 0) == iota((128, 128), 1)
     n = rows // 128
@@ -390,10 +404,10 @@
     rows = tall - STAT_ROWS
     return pl.pallas_call(
         functools.partial(merge_kernel, len(parts)),
-        grid=(devices,),
+        grid=(devices // 2,),
         in_specs=[pl.BlockSpec(memory_space=pltpu.SMEM)]
-        + [pl.BlockSpec((None, tall, width), lambda i: (i, 0, 0))] * len(parts),
-        out_specs=pl.BlockSpec((None, rows, width), lambda i: (i, 0, 0)),
+        + [pl.BlockSpec((2, tall, width), lambda i: (i, 0, 0))] * len(parts),
+        out_specs=pl.BlockSpec((2, rows, width), lambda i: (i, 0, 0)),
         out_shape=jax.ShapeDtypeStruct((devices, rows, width), jnp.bfloat16),
         compiler_params=params(),
         name="merge_parts",
@@ -468,6 +482,8 @@
     def after(array, *others):
         return lax.optimization_barrier((array, *others))
 
+    v_heads = heads_first(value_rows)
+    v_heads, cluster_ids = after(v_heads, cluster_ids)
     slots, counts = rank_tokens(cluster_ids)
     facts = lax.all_gather(jnp.concatenate([slots, counts], axis=1), AXES)
     facts = lax.dynamic_index_in_dim(facts, place, 1, keepdims=False)
@@ -477,23 +493,11 @@
         return [(2 * j + side, 2 * (j - shift) + 1) for j in range(shift, couples)]
 
     pair_routes = [(2 * j, 2 * j + 1) for j in range(couples)]
-    keys = swap(heads_first(key_rows))
-    pair_keys = move(keys, pair_routes)
-    q_heads, keys = after(heads_first(query_rows), keys)
-    queries = swap(q_heads)
 
     def visit(queries, shift):
         first = move(queries, visit_routes(shift, 0))
         queries, first = after(queries, first)
         return [first, move(queries, visit_routes(shift, 1))]
-
-    visitors = visit(queries, 1) if couples > 1 else []
-    v_heads, queries = after(heads_first(value_rows), queries)
-    values = swap(v_heads)
-    pair_values = move(values, pair_routes)
-    past = [key_rows[:, :local_width], value_rows[:, :local_width]]
-    *past, pair_values = after(past[0], past[1], pair_values)
-    past = [lax.ppermute(m, AXES, [(i, i + 1) for i in range(device_count - 1)]) for m in past]
 
     def facts_of(index):
         return lax.dynamic_index_in_dim(facts, index, 0, keepdims=False)
@@ -513,16 +517,38 @@
         [bias_of(own_facts[:, rows:]), jnp.where(is_odd, bias_of(pair_facts[:, rows:]), NEGATIVE)],
         axis=1,
     )
-    own_q, own_k, own_v = dispatch(
-        own_facts[:, :rows], [(queries, None), (keys, None), (values, None)], "dispatch_own"
+
+    def one(slots, array, name):
+        return dispatch(slots, [(array, None)], name)[0]
+
+    own_slots, pair_slots, homes = own_facts[:, :rows], pair_facts[:, :rows], visit_slots(1)
+    raw_values = move(v_heads, pair_routes)
+    keys = swap(heads_first(key_rows))
+    pair_keys = move(keys, pair_routes)
+    q_heads, keys = after(heads_first(query_rows), keys)
+    queries = swap(q_heads)
+    visitors = [move(queries, visit_routes(1, 0))] if couples > 1 else []
+    v_heads, queries = after(v_heads, queries)
+    values = swap(v_heads)
+    own_q, own_k = dispatch(own_slots, [(queries, None), (keys, None)], "dispatch_queries_keys")
+    raw_values, values, own_k = after(raw_values, values, own_k)
+    pair_values = swap(raw_values)
+    *past, own_k = after(key_rows, value_rows, own_k)
+    past = [m[:, :local_width] for m in past]
+    past = [lax.ppermute(m, AXES, [(i, i + 1) for i in range(device_count - 1)]) for m in past]
+    values, own_q = after(values, own_q)
+    own_v = one(own_slots, values, "dispatch_values")
+    if visitors:
+        queries, visitors[0], own_v = after(queries, visitors[0], own_v)
+        visitors.append(move(queries, visit_routes(1, 1)))
+    asked = []
+    if visitors:
+        visitors[0], own_v = after(visitors[0], own_v)
+        asked = [one(homes[0], visitors[0], "dispatch_visit")]
+        pair_values, asked[0] = after(pair_values, asked[0])
+    pair_k, pair_v = dispatch(
+        pair_slots, [(pair_keys, None), (pair_values, None)], "dispatch_pair"
     )
-    (pair_k,) = dispatch(pair_facts[:, :rows], [(pair_keys, None)], "dispatch_pair_keys")
-    homes = visit_slots(1)
-    asked = []
-    if couples > 1:
-        asked = list(dispatch(homes[0], [(visitors[0], None)], "dispatch_visit"))
-        pair_values, pair_k, own_q, asked[0] = after(pair_values, pair_k, own_q, asked[0])
-    (pair_v,) = dispatch(pair_facts[:, :rows], [(pair_values, None)], "dispatch_pair_values")
     kept = (bias, own_k, own_v, pair_k, pair_v)
 
     parts, valid = [], [jnp.int32(1)]
@@ -531,10 +557,10 @@
         if shift > 1:
             queries, parts[-1][-1] = after(queries, parts[-1][-1])
             visitors = visit(queries, shift)
-            asked = list(dispatch(homes[0], [(visitors[0], None)], "dispatch_visit"))
+            asked = [one(homes[0], visitors[0], "dispatch_visit")]
         for side in range(2):
             if side == 1:
-                asked = dispatch(homes[1], [(visitors[1], None)], "dispatch_visit")
+                asked = [one(homes[1], visitors[1], "dispatch_visit")]
             found = list(answer(*kept, asked[0], homes[side], False, "answer_visit"))
             if side == 0:
                 visitors[1], found[0] = after(visitors[1], found[0])
@@ -543,8 +569,8 @@
             routes = [(b, a) for a, b in visit_routes(shift, side)]
             back = []
             for half in range(HALVES):
-                if half:
-                    found[half], back[-1] = after(found[half], back[-1])
+                if half and side:
+                    found[half], parts[-1][-1] = after(found[half], parts[-1][-1])
                 back.append(move(found[half], routes))
             parts.append(back)
             valid.append(((plane // 2 >= shift) & (plane % 2 == side)).astype(jnp.int32))

time: 359 us -> 349 us (0.972)
  starting transfers between devices: 47.7 us -> 60.2 us
  Pallas kernels: 199 us -> 187 us
  waiting for transfers between devices: 79.3 us -> 71.8 us
  local copies, waits for them, and re-layouts: 15.5 us -> 11.4 us
    all_to_all x5 -> x6, waiting for transfers between devices: 61.6 us -> 47.5 us  [swap(): lax.all_to_all(array, AXES, split_axis=0, concat_axis=0, tiled=True, axis...]
    pallas_call x5, Pallas kernels: 70.8 us -> 62.3 us  [dispatch(): pl.pallas_call(functools.partial(dispatch_kernel, count), grid=(pairs,),...]
    all_gather x1, waiting for transfers between devices: 0.01 us -> 8.47 us  [on_device(): facts = lax.all_gather(jnp.concatenate([slots, counts], axis=1), AXES)]
    ppermute x8, starting transfers between devices: 22.3 us -> 30.5 us  [move(): return lax.ppermute(array, AXES, pairs)]
    reshape x7 -> x4, local copies, waits for them, and re-layouts: 7.28 us -> 2.5 us  [dispatch(): operands = [slots.reshape(pairs, 2, rows)]]
    all_to_all x5 -> x6, starting transfers between devices: 19.6 us -> 24 us  [swap(): lax.all_to_all(array, AXES, split_axis=0, concat_axis=0, tiled=True, axis...]
    pallas_call x2, Pallas kernels: 13.8 us -> 9.46 us  [merge(): pl.pallas_call(functools.partial(merge_kernel, len(parts)), grid=(devices...]
  transfers between devices with their start and end apart: 16 -> 17, of which waited for: 6 -> 5; matrix products, arithmetic and copies ran while one was open for 5% -> 3% of each run, Pallas kernels for 54% -> 52%
where the time goes in v3:
time: 349 us; the launch traced here: 347 us
  Pallas kernels  187 us (54%)
  waiting for transfers between devices  71.8 us (21%)
  starting transfers between devices  60.2 us (17%)
  between operations  13.8 us (4%)
  local copies, waits for them, and re-layouts  11.4 us (3%)
    pallas_call x3, Pallas kernels, answer(): pl.pallas_call(functools.partial(answer_kernel, own, steps), grid=(steps...  71 us
    pallas_call x5, Pallas kernels, dispatch(): pl.pallas_call(functools.partial(dispatch_kernel, count), grid=(pairs,),...  62.3 us
    all_to_all x6, waiting for transfers between devices, swap(): lax.all_to_all(array, AXES, split_axis=0, concat_axis=0, tiled=True, axis...  47.5 us
    ppermute x8, starting transfers between devices, move(): return lax.ppermute(array, AXES, pairs)  30.5 us
    all_to_all x6, starting transfers between devices, swap(): lax.all_to_all(array, AXES, split_axis=0, concat_axis=0, tiled=True, axis...  24 us
    pallas_call x1, Pallas kernels, window_heads(): pl.pallas_call(window_kernel, grid=(HEADS_L,), in_specs=[pl.BlockSpec(mem...  21.7 us
    ppermute x8, waiting for transfers between devices, move(): return lax.ppermute(array, AXES, pairs)  15.8 us
    pallas_call x3, Pallas kernels, heads_first(): pl.pallas_call(heads_kernel, grid=(rows // block,), in_specs=[pl.BlockSpe...  11.8 us
  transfers between devices with their start and end apart: 17, of which 5 were waited for; matrix products, arithmetic and copies ran while one was open for 3% of the time, Pallas kernels for 52%

profile of v3, /device:TPU:24, one launch (start us, length us, event | category | flops | bytes accessed | tf_op | source)
XLA Modules:
  0.0 347.4 jit_solution(10192791072244256429)
XLA Ops:
  6.5 4.0 %heads_first.5 = bf16[8,1024,128]{2,1,0:T(8,128)(2,1)} custom-call(bf16[1024,2048]{1,0:T(8,128)(2,1)} %own_k.1), custom_call_target="tpu_custom_call" | custom-call | tf_op jit(solution)/shard_map/heads_first/pallas_call | solution.py:450
  10.5 3.7 %all-to-all-start = ((bf16[8,1024,128]{2,1,0:T(8,128)(2,1)}), bf16[8,1024,128]{2,1,0:T(8,128)(2,1)S(1)}, u32[]{:S(2)}, u32[]{:S(2)}) async-start(bf16[8,1024,128]{2,1,0:T(8,128)(2,1)} %heads_first.5), calls=%async_computation | async-start | bytes 4194304 | tf_op jit(solution)/shard_map/all_to_all | solution.py:474
  14.2 0.0 all-gather.3.cloned.1.call-start
  14.3 4.0 %heads_first.3 = bf16[8,1024,128]{2,1,0:T(8,128)(2,1)} custom-call(bf16[1024,2048]{1,0:T(8,128)(2,1)} %own_v.1), custom_call_target="tpu_custom_call" | custom-call | tf_op jit(solution)/shard_map/heads_first/pallas_call | solution.py:450
  18.2 6.9 %rank_tokens.1 = (s32[8,1024]{1,0:T(8,128)}, s32[8,256]{1,0:T(8,128)}) custom-call(s32[8,1024]{1,0:T(8,128)} %ids_ref), custom_call_target="tpu_custom_call" | custom-call | tf_op jit(solution)/shard_map/rank_tokens/pallas_call | solution.py:56
  25.1 1.4 pad_add_fusion
  26.5 0.0 all-gather.3.cloned.1.call-update
  26.5 3.9 %heads_first.4 = bf16[8,1024,128]{2,1,0:T(8,128)(2,1)} custom-call(bf16[1024,2048]{1,0:T(8,128)(2,1)} %q_ref.1), custom_call_target="tpu_custom_call" | custom-call | tf_op jit(solution)/shard_map/heads_first/pallas_call | solution.py:450
  30.4 9.8 %all-to-all-done.refs_1_ = bf16[8,1024,128]{2,1,0:T(8,128)(2,1)S(1)} async-done(((bf16[8,1024,128]{2,1,0:T(8,128)(2,1)}), bf16[8,1024,128]{2,1,0:T(8,128)(2,1)S(1)}, u32[]{:S(2)}, u32[]{:S(2)}) %all-to-all-start) | async-done | bytes 2097184 | tf_op jit(solution)/shard_map/all_to_all | solution.py:474
  40.2 4.4 %all-to-all-start.1 = ((bf16[8,1024,128]{2,1,0:T(8,128)(2,1)}), bf16[8,1024,128]{2,1,0:T(8,128)(2,1)}, u32[]{:S(2)}, u32[]{:S(2)}) async-start(bf16[8,1024,128]{2,1,0:T(8,128)(2,1)} %heads_first.4), calls=%async_computation.1 | async-start | bytes 4194304 | tf_op jit(solution)/shard_map/all_to_all | solution.py:474
  44.6 1.3 collective-permute-start
  45.9 25.5 %all-to-all-done.1.refs_0_ = bf16[8,1024,128]{2,1,0:T(8,128)(2,1)} async-done(((bf16[8,1024,128]{2,1,0:T(8,128)(2,1)}), bf16[8,1024,128]{2,1,0:T(8,128)(2,1)}, u32[]{:S(2)}, u32[]{:S(2)}) %all-to-all-start.1) | async-done | bytes 2097184 | tf_op jit(solution)/shard_map/all_to_all | solution.py:474
  71.4 4.4 %all-to-all-start.2 = ((bf16[8,1024,128]{2,1,0:T(8,128)(2,1)}), bf16[8,1024,128]{2,1,0:T(8,128)(2,1)}, u32[]{:S(2)}, u32[]{:S(2)}) async-start(bf16[8,1024,128]{2,1,0:T(8,128)(2,1)} %heads_first.3), calls=%async_computation.2 | async-start | bytes 4194304 | tf_op jit(solution)/shard_map/all_to_all | solution.py:474
  75.9 0.1 lt.76
  76.0 0.7 add_convert_fusion.valid_ref
  76.7 1.3 collective-permute-start.2
  77.9 8.5 %all-gather.3.cloned.1.call-done = s32[256,1280]{1,0:T(8,128)} async-done(((s32[8,1280]{1,0:T(8,128)}), s32[256,1280]{1,0:T(8,128)}) %all-gather.3.cloned.1.call-update) | async-done | bytes 1310736 | tf_op jit(solution)/shard_map/all_gather | solution.py:488
  86.4 1.4 constant_dynamic-slice_fusion
  87.9 0.6 reshape.32.slot_ref
  88.5 0.6 reshape.34.slot_ref
  89.2 0.6 reshape.33.slot_ref
  89.8 2.0 collective-permute-start.1
  91.8 12.7 %dispatch_queries_keys.1 = (bf16[256,4,16,128]{3,2,1,0:T(8,128)(2,1)}, bf16[256,4,16,128]{3,2,1,0:T(8,128)(2,1)}) custom-call(s32[4,2,1024]{2,1,0:T(2,128)} %reshape.32.slot_ref, bf16[8,1024,128]{2,1,0:T(8,128)(2,1)} %all-to-all-done.1.refs_0_, bf16[8,1024,128]{2,1,0:T(8,128)(2,1)} %copy-done.4), custom_call_target="tpu_custom_call" | custom-call | flops 8589934592 | bytes 24000000 | tf_op jit(solution)/shard_map/dispatch_queries_keys/pallas_call | solution.py:139
  104.6 0.0 collective-permute-done
  104.6 4.3 %all-to-all-start.3 = ((bf16[8,1024,128]{2,1,0:T(8,128)(2,1)}), bf16[8,1024,128]{2,1,0:T(8,128)(2,1)}, u32[]{:S(2)}, u32[]{:S(2)}) async-start(bf16[8,1024,128]{2,1,0:T(8,128)(2,1)} %collective-permute-done), calls=%async_computation.3 | async-start | bytes 4194304 | tf_op jit(solution)/shard_map/all_to_all | solution.py:474
  109.0 0.1 copy.10
  109.1 0.1 copy.9
  109.2 0.6 reshape.35.slot_ref
  109.8 0.0 copy-start
  109.9 12.4 %dispatch_values.1.own_v = bf16[256,4,16,128]{3,2,1,0:T(8,128)(2,1)} custom-call(s32[4,2,1024]{2,1,0:T(2,128)} %reshape.32.slot_ref, bf16[8,1024,128]{2,1,0:T(8,128)(2,1)} %all-to-all-done.2.refs_0_), custom_call_target="tpu_custom_call" | custom-call | flops 4294967296 | bytes 12000000 | tf_op jit(solution)/shard_map/dispatch_values/pallas_call | solution.py:139
  122.3 21.6 %collective-permute-start.3 = (bf16[8,1024,128]{2,1,0:T(8,128)(2,1)}, bf16[8,1024,128]{2,1,0:T(8,128)(2,1)}, u32[]{:S(2)}, u32[]{:S(2)}) collective-permute-start(bf16[8,1024,128]{2,1,0:T(8,128)(2,1)} %all-to-all-done.1.refs_0_), channel_id=1, source_target_pairs={{24,8},{25,9},{26,10},{27,11},{28,12},{29,13},{30,14},{31,15}} | collective-permute-start | bytes 6291464 | tf_op jit(solution)/shard_map/ppermute | solution.py:480
  143.9 0.7 pad_maximum_fusion.bias_ref
  144.7 1.5 slice.32
  146.2 2.0 collective-permute-start.5
  148.3 1.6 slice.33
  149.8 3.7 %collective-permute-start.6 = (bf16[1024,1024]{1,0:T(8,128)(2,1)}, bf16[1024,1024]{1,0:T(8,128)(2,1)}, u32[]{:S(2)}, u32[]{:S(2)}) collective-permute-start(bf16[1024,1024]{1,0:T(8,128)(2,1)} %slice.33), channel_id=1, source_target_pairs={{0,1},{1,2},{2,3},{3,4},{4,5},{5,6},{6,7},{7,8},{8,9},{9,10},{10,1... | collective-permute-start | bytes 6291464 | tf_op jit(solution)/shard_map/ppermute | solution.py:538
  153.5 12.2 %dispatch_visit.2.query = bf16[256,4,16,128]{3,2,1,0:T(8,128)(2,1)} custom-call(s32[4,2,1024]{2,1,0:T(2,128)} %reshape.34.slot_ref, bf16[8,1024,128]{2,1,0:T(8,128)(2,1)} %collective-permute-done.1.refs_0_), custom_call_target="tpu_custom_call" | custom-call | flops 4294967296 | bytes 12000000 | tf_op jit(solution)/shard_map/dispatch_visit/pallas_call | solution.py:139
  165.7 0.0 all-to-all-done.3.refs_1_
  165.7 0.0 collective-permute-done.2.refs_0_
  165.7 12.7 %dispatch_pair.1 = (bf16[256,4,16,128]{3,2,1,0:T(8,128)(2,1)}, bf16[256,4,16,128]{3,2,1,0:T(8,128)(2,1)}) custom-call(s32[4,2,1024]{2,1,0:T(2,128)} %reshape.33.slot_ref, bf16[8,1024,128]{2,1,0:T(8,128)(2,1)} %collective-permute-done.2.refs_0_, bf16[8,1024,128]{2,1,0:T(8,128)(2,1)} %all-to-all-done.3.refs_1_), custom_call_target="tpu_custom_call" | custom-call | flops 8589934592 | bytes 24000000 | tf_op jit(solution)/shard_map/dispatch_pair/pallas_call | solution.py:139
  178.4 23.6 %answer_visit.2 = (bf16[8,528,128]{2,1,0:T(8,128)(2,1)}, bf16[8,528,128]{2,1,0:T(8,128)(2,1)}) custom-call(f32[256,128]{1,0:T(8,128)} %pad_maximum_fusion.bias_ref, bf16[256,4,16,128]{3,2,1,0:T(8,128)(2,1)} %get-tuple-element.63.own_k, bf16[256,4,16,128]{3,2,1,0:T(8,128)(2,1)} %dispatch_values.1.own_v, bf16[256,4,16,128]{3,2,1,0:T(8,128)(2,1)} %get-tuple-element.71.pair_k, ...), custom_call_target="tpu_custom_call" | custom-call | flops 8589934592 | bytes 30000000 | tf_op jit(solution)/shard_map/answer_visit/pallas_call | solution.py:290
  202.1 0.7 collective-permute-start.7
  202.8 0.0 collective-permute-done.3.refs_0_
  202.8 12.2 %dispatch_visit.3.query = bf16[256,4,16,128]{3,2,1,0:T(8,128)(2,1)} custom-call(s32[4,2,1024]{2,1,0:T(2,128)} %reshape.35.slot_ref, bf16[8,1024,128]{2,1,0:T(8,128)(2,1)} %collective-permute-done.3.refs_0_), custom_call_target="tpu_custom_call" | custom-call | flops 4294967296 | bytes 12000000 | tf_op jit(solution)/shard_map/dispatch_visit/pallas_call | solution.py:139
  215.0 23.6 %answer_visit.3 = (bf16[8,528,128]{2,1,0:T(8,128)(2,1)}, bf16[8,528,128]{2,1,0:T(8,128)(2,1)}) custom-call(f32[256,128]{1,0:T(8,128)} %pad_maximum_fusion.bias_ref, bf16[256,4,16,128]{3,2,1,0:T(8,128)(2,1)} %get-tuple-element.63.own_k, bf16[256,4,16,128]{3,2,1,0:T(8,128)(2,1)} %dispatch_values.1.own_v, bf16[256,4,16,128]{3,2,1,0:T(8,128)(2,1)} %get-tuple-element.71.pair_k, ...), custom_call_target="tpu_custom_call" | custom-call | flops 8589934592 | bytes 30000000 | tf_op jit(solution)/shard_map/answer_visit/pallas_call | solution.py:290
  238.6 1.3 collective-permute-start.4
  239.9 1.0 collective-permute-start.9
  240.9 23.7 %answer_own.1 = (bf16[8,528,128]{2,1,0:T(8,128)(2,1)}, bf16[8,528,128]{2,1,0:T(8,128)(2,1)}) custom-call(f32[256,128]{1,0:T(8,128)} %pad_maximum_fusion.bias_ref, bf16[256,4,16,128]{3,2,1,0:T(8,128)(2,1)} %get-tuple-element.63.own_k, bf16[256,4,16,128]{3,2,1,0:T(8,128)(2,1)} %dispatch_values.1.own_v, bf16[256,4,16,128]{3,2,1,0:T(8,128)(2,1)} %get-tuple-element.71.pair_k, ...), custom_call_target="tpu_custom_call" | custom-call | flops 8589934592 | bytes 30000000 | tf_op jit(solution)/shard_map/answer_own/pallas_call | solution.py:290
  264.6 0.0 collective-permute-done.5.past_k
  264.6 1.3 collective-permute-start.8
  265.9 21.7 %window_heads.1.base_ref = bf16[1024,2048]{1,0:T(8,128)(2,1)} custom-call(s32[1]{0:T(128)} %bitcast.9.first_ref, bf16[1024,2048]{1,0:T(8,128)(2,1)} %q_ref.1, bf16[1024,2048]{1,0:T(8,128)(2,1)} %own_k.1, bf16[1024,2048]{1,0:T(8,128)(2,1)} %own_v.1, bf16[1024,1024]{1,0:T(8,128)(2,1)} %collective-permute-done.5.past_k, ...), custom_call_target="tpu_custom_call" | custom-call | flops 10737418240 | bytes 14000000 | tf_op jit(solution)/shard_map/window_heads/pallas_call | solution.py:356
  287.6 0.0 collective-permute-done.4.refs_2_
  287.7 1.0 copy-done.6
  288.6 1.0 copy-done.7
  289.7 4.7 %merge_parts.3 = bf16[8,512,128]{2,1,0:T(8,128)(2,1)} custom-call(s32[3]{0:T(128)} %add_convert_fusion.valid_ref, bf16[8,528,128]{2,1,0:T(8,128)(2,1)} %get-tuple-element.90.refs_0_, bf16[8,528,128]{2,1,0:T(8,128)(2,1)} %copy-done.7, bf16[8,528,128]{2,1,0:T(8,128)(2,1)} %copy-done.6), custom_call_target="tpu_custom_call" | custom-call | tf_op jit(solution)/shard_map/merge_parts/pallas_call | solution.py:405
  294.4 3.6 %all-to-all-start.4 = ((bf16[8,512,128]{2,1,0:T(8,128)(2,1)}), bf16[8,512,128]{2,1,0:T(8,128)(2,1)S(1)}, u32[]{:S(2)}, u32[]{:S(2)}) async-start(bf16[8,512,128]{2,1,0:T(8,128)(2,1)} %merge_parts.3), calls=%async_computation.4 | async-start | bytes 2097152 | tf_op jit(solution)/shard_map/all_to_all | solution.py:474
  298.0 15.8 %collective-permute-done.8.refs_2_ = bf16[8,528,128]{2,1,0:T(8,128)(2,1)S(1)} collective-permute-done((bf16[8,528,128]{2,1,0:T(8,128)(2,1)}, bf16[8,528,128]{2,1,0:T(8,128)(2,1)S(1)}, u32[]{:S(2)}, u32[]{:S(2)}) %collective-permute-start.8) | collective-permute-done | bytes 1081376 | tf_op jit(solution)/shard_map/ppermute | solution.py:480
  313.8 1.0 copy-done.8
  314.8 4.7 %merge_parts.2 = bf16[8,512,128]{2,1,0:T(8,128)(2,1)} custom-call(s32[3]{0:T(128)} %add_convert_fusion.valid_ref, bf16[8,528,128]{2,1,0:T(8,128)(2,1)} %get-tuple-element.85.refs_0_, bf16[8,528,128]{2,1,0:T(8,128)(2,1)} %copy-done.5, bf16[8,528,128]{2,1,0:T(8,128)(2,1)} %copy-done.8), custom_call_target="tpu_custom_call" | custom-call | tf_op jit(solution)/shard_map/merge_parts/pallas_call | solution.py:405
  319.5 3.6 %all-to-all-start.5 = ((bf16[8,512,128]{2,1,0:T(8,128)(2,1)}), bf16[8,512,128]{2,1,0:T(8,128)(2,1)S(1)}, u32[]{:S(2)}, u32[]{:S(2)}) async-start(bf16[8,512,128]{2,1,0:T(8,128)(2,1)} %merge_parts.2), calls=%async_computation.5 | async-start | bytes 2097152 | tf_op jit(solution)/shard_map/all_to_all | solution.py:474
  323.1 2.2 place_heads.2.base_ref
  325.2 12.2 %all-to-all-done.5.heads_ref = bf16[8,512,128]{2,1,0:T(8,128)(2,1)S(1)} async-done(((bf16[8,512,128]{2,1,0:T(8,128)(2,1)}), bf16[8,512,128]{2,1,0:T(8,128)(2,1)S(1)}, u32[]{:S(2)}, u32[]{:S(2)}) %all-to-all-start.5) | async-done | bytes 1048608 | tf_op jit(solution)/shard_map/all_to_all | solution.py:474
  337.4 1.0 copy-done.3
  338.4 2.2 place_heads.3
  (32 shorter events, 0.1 us)
Async XLA Ops:
  10.5 29.7 %all-to-all-start = ((bf16[8,1024,128]{2,1,0:T(8,128)(2,1)}), bf16[8,1024,128]{2,1,0:T(8,128)(2,1)S(1)}, u32[]{:S(2)}, u32[]{:S(2)}) async-start(bf16[8,1024,128]{2,1,0:T(8,128)(2,1)} %heads_first.5), calls=%async_computation | async-start | bytes 4194304 | tf_op jit(solution)/shard_map/all_to_all | solution.py:474
  14.2 72.2 %all-gather.3.cloned.1.call-start = ((), (), s32[]{:S(2)}) async-start(), calls=%async_computation.6 | async-start | bytes 1351680 | tf_op jit(solution)/shard_map/all_gather | solution.py:488
  40.2 36.5 %copy-start.4 = (bf16[8,1024,128]{2,1,0:T(8,128)(2,1)}, bf16[8,1024,128]{2,1,0:T(8,128)(2,1)S(1)}, u32[]{:S(2)}) copy-start(bf16[8,1024,128]{2,1,0:T(8,128)(2,1)S(1)} %all-to-all-done.refs_1_) | copy-start | bytes 6291460
  40.2 31.2 %all-to-all-start.1 = ((bf16[8,1024,128]{2,1,0:T(8,128)(2,1)}), bf16[8,1024,128]{2,1,0:T(8,128)(2,1)}, u32[]{:S(2)}, u32[]{:S(2)}) async-start(bf16[8,1024,128]{2,1,0:T(8,128)(2,1)} %heads_first.4), calls=%async_computation.1 | async-start | bytes 4194304 | tf_op jit(solution)/shard_map/all_to_all | solution.py:474
  44.6 60.0 %collective-permute-start = (bf16[8,1024,128]{2,1,0:T(8,128)(2,1)}, bf16[8,1024,128]{2,1,0:T(8,128)(2,1)}, u32[]{:S(2)}, u32[]{:S(2)}) collective-permute-start(bf16[8,1024,128]{2,1,0:T(8,128)(2,1)} %heads_first.3), channel_id=1, source_target_pairs={{0,8},{1,9},{2,10},{3,11},{4,12},{5,13},{6,14},{7,15},{16,24},{17,... | collective-permute-start | bytes 6291464 | tf_op jit(solution)/shard_map/ppermute | solution.py:480
  71.4 33.2 %all-to-all-start.2 = ((bf16[8,1024,128]{2,1,0:T(8,128)(2,1)}), bf16[8,1024,128]{2,1,0:T(8,128)(2,1)}, u32[]{:S(2)}, u32[]{:S(2)}) async-start(bf16[8,1024,128]{2,1,0:T(8,128)(2,1)} %heads_first.3), calls=%async_computation.2 | async-start | bytes 4194304 | tf_op jit(solution)/shard_map/all_to_all | solution.py:474
  76.7 89.0 %collective-permute-start.2 = (bf16[8,1024,128]{2,1,0:T(8,128)(2,1)S(1)}, bf16[8,1024,128]{2,1,0:T(8,128)(2,1)}, u32[]{:S(2)}, u32[]{:S(2)}) collective-permute-start(bf16[8,1024,128]{2,1,0:T(8,128)(2,1)S(1)} %all-to-all-done.refs_1_), channel_id=1, source_target_pairs={{0,8},{1,9},{2,10},{3,11},{4,12},{5,13},{6,14},{7,15},{16,24},{17,... | collective-permute-start | bytes 6291464 | tf_op jit(solution)/shard_map/ppermute | solution.py:480
  89.8 32.5 %collective-permute-start.1 = (bf16[8,1024,128]{2,1,0:T(8,128)(2,1)}, bf16[8,1024,128]{2,1,0:T(8,128)(2,1)}, u32[]{:S(2)}, u32[]{:S(2)}) collective-permute-start(bf16[8,1024,128]{2,1,0:T(8,128)(2,1)} %all-to-all-done.1.refs_0_), channel_id=1, source_target_pairs={{16,8},{17,9},{18,10},{19,11},{20,12},{21,13},{22,14},{23,15}} | collective-permute-start | bytes 6291464 | tf_op jit(solution)/shard_map/ppermute | solution.py:480
  104.6 61.1 %all-to-all-start.3 = ((bf16[8,1024,128]{2,1,0:T(8,128)(2,1)}), bf16[8,1024,128]{2,1,0:T(8,128)(2,1)}, u32[]{:S(2)}, u32[]{:S(2)}) async-start(bf16[8,1024,128]{2,1,0:T(8,128)(2,1)} %collective-permute-done), calls=%async_computation.3 | async-start | bytes 4194304 | tf_op jit(solution)/shard_map/all_to_all | solution.py:474
  109.8 34.8 %copy-start = (bf16[1024,2048]{1,0:T(8,128)(2,1)S(1)}, bf16[1024,2048]{1,0:T(8,128)(2,1)}, u32[]{:S(2)}) copy-start(bf16[1024,2048]{1,0:T(8,128)(2,1)} %own_k.1) | copy-start | bytes 12582916
  122.3 80.5 %collective-permute-start.3 = (bf16[8,1024,128]{2,1,0:T(8,128)(2,1)}, bf16[8,1024,128]{2,1,0:T(8,128)(2,1)}, u32[]{:S(2)}, u32[]{:S(2)}) collective-permute-start(bf16[8,1024,128]{2,1,0:T(8,128)(2,1)} %all-to-all-done.1.refs_0_), channel_id=1, source_target_pairs={{24,8},{25,9},{26,10},{27,11},{28,12},{29,13},{30,14},{31,15}} | collective-permute-start | bytes 6291464 | tf_op jit(solution)/shard_map/ppermute | solution.py:480
  144.7 3.6 %copy-start.1 = (bf16[1024,2048]{1,0:T(8,128)(2,1)S(1)}, bf16[1024,2048]{1,0:T(8,128)(2,1)}, u32[]{:S(2)}) copy-start(bf16[1024,2048]{1,0:T(8,128)(2,1)} %own_v.1) | copy-start | bytes 12582916
  146.2 118.4 %collective-permute-start.5 = (bf16[1024,1024]{1,0:T(8,128)(2,1)}, bf16[1024,1024]{1,0:T(8,128)(2,1)}, u32[]{:S(2)}, u32[]{:S(2)}) collective-permute-start(bf16[1024,1024]{1,0:T(8,128)(2,1)} %slice.32), channel_id=1, source_target_pairs={{0,1},{1,2},{2,3},{3,4},{4,5},{5,6},{6,7},{7,8},{8,9},{9,10},{10,1... | collective-permute-start | bytes 6291464 | tf_op jit(solution)/shard_map/ppermute | solution.py:538
  149.8 116.1 %collective-permute-start.6 = (bf16[1024,1024]{1,0:T(8,128)(2,1)}, bf16[1024,1024]{1,0:T(8,128)(2,1)}, u32[]{:S(2)}, u32[]{:S(2)}) collective-permute-start(bf16[1024,1024]{1,0:T(8,128)(2,1)} %slice.33), channel_id=1, source_target_pairs={{0,1},{1,2},{2,3},{3,4},{4,5},{5,6},{6,7},{7,8},{8,9},{9,10},{10,1... | collective-permute-start | bytes 6291464 | tf_op jit(solution)/shard_map/ppermute | solution.py:538
  202.1 62.5 %collective-permute-start.7 = (bf16[8,528,128]{2,1,0:T(8,128)(2,1)}, bf16[8,528,128]{2,1,0:T(8,128)(2,1)S(1)}, u32[]{:S(2)}, u32[]{:S(2)}) collective-permute-start(bf16[8,528,128]{2,1,0:T(8,128)(2,1)} %get-tuple-element.87), channel_id=1, source_target_pairs={{8,16},{9,17},{10,18},{11,19},{12,20},{13,21},{14,22},{15,23}} | collective-permute-start | bytes 3244040 | tf_op jit(solution)/shard_map/ppermute | solution.py:480
  215.0 24.9 %copy-start.9 = (bf16[8,528,128]{2,1,0:T(8,128)(2,1)S(1)}, bf16[8,528,128]{2,1,0:T(8,128)(2,1)}, u32[]{:S(2)}) copy-start(bf16[8,528,128]{2,1,0:T(8,128)(2,1)} %get-tuple-element.91) | copy-start | bytes 3244036
  238.6 49.0 %collective-permute-start.4 = (bf16[8,528,128]{2,1,0:T(8,128)(2,1)}, bf16[8,528,128]{2,1,0:T(8,128)(2,1)S(1)}, u32[]{:S(2)}, u32[]{:S(2)}) collective-permute-start(bf16[8,528,128]{2,1,0:T(8,128)(2,1)} %get-tuple-element.78), channel_id=1, source_target_pairs={{8,24},{9,25},{10,26},{11,27},{12,28},{13,29},{14,30},{15,31}} | collective-permute-start | bytes 3244040 | tf_op jit(solution)/shard_map/ppermute | solution.py:480
  239.9 47.7 %collective-permute-start.9 = (bf16[8,528,128]{2,1,0:T(8,128)(2,1)S(1)}, bf16[8,528,128]{2,1,0:T(8,128)(2,1)S(1)}, u32[]{:S(2)}, u32[]{:S(2)}) collective-permute-start(bf16[8,528,128]{2,1,0:T(8,128)(2,1)S(1)} %copy-done.9), channel_id=1, source_target_pairs={{8,16},{9,17},{10,18},{11,19},{12,20},{13,21},{14,22},{15,23}} | collective-permute-start | bytes 3244040 | tf_op jit(solution)/shard_map/ppermute | solution.py:480
  264.6 23.0 %copy-start.5 = (bf16[8,528,128]{2,1,0:T(8,128)(2,1)}, bf16[8,528,128]{2,1,0:T(8,128)(2,1)S(1)}, u32[]{:S(2)}) copy-start(bf16[8,528,128]{2,1,0:T(8,128)(2,1)S(1)} %collective-permute-done.7.refs_1_) | copy-start | bytes 3244036
  264.6 49.1 %collective-permute-start.8 = (bf16[8,528,128]{2,1,0:T(8,128)(2,1)}, bf16[8,528,128]{2,1,0:T(8,128)(2,1)S(1)}, u32[]{:S(2)}, u32[]{:S(2)}) collective-permute-start(bf16[8,528,128]{2,1,0:T(8,128)(2,1)} %get-tuple-element.89), channel_id=1, source_target_pairs={{8,24},{9,25},{10,26},{11,27},{12,28},{13,29},{14,30},{15,31}} | collective-permute-start | bytes 3244040 | tf_op jit(solution)/shard_map/ppermute | solution.py:480
  287.6 1.0 copy-start.6
  288.6 1.0 copy-start.7
  294.4 25.1 %all-to-all-start.4 = ((bf16[8,512,128]{2,1,0:T(8,128)(2,1)}), bf16[8,512,128]{2,1,0:T(8,128)(2,1)S(1)}, u32[]{:S(2)}, u32[]{:S(2)}) async-start(bf16[8,512,128]{2,1,0:T(8,128)(2,1)} %merge_parts.3), calls=%async_computation.4 | async-start | bytes 2097152 | tf_op jit(solution)/shard_map/all_to_all | solution.py:474
  313.8 1.0 copy-start.8
  319.5 3.6 %copy-start.2 = (bf16[8,512,128]{2,1,0:T(8,128)(2,1)}, bf16[8,512,128]{2,1,0:T(8,128)(2,1)S(1)}, u32[]{:S(2)}) copy-start(bf16[8,512,128]{2,1,0:T(8,128)(2,1)S(1)} %all-to-all-done.4.heads_ref) | copy-start | bytes 3145732
  319.5 18.0 %all-to-all-start.5 = ((bf16[8,512,128]{2,1,0:T(8,128)(2,1)}), bf16[8,512,128]{2,1,0:T(8,128)(2,1)S(1)}, u32[]{:S(2)}, u32[]{:S(2)}) async-start(bf16[8,512,128]{2,1,0:T(8,128)(2,1)} %merge_parts.2), calls=%async_computation.5 | async-start | bytes 2097152 | tf_op jit(solution)/shard_map/all_to_all | solution.py:474
  337.4 1.0 copy-start.3
Sparse Core Ops, SparseCore 0:
  26.7 59.7 all-gather.2

commit v4 on v3

--- a/solution.py
+++ b/solution.py
@@ -535,7 +535,10 @@
     pair_values = swap(raw_values)
     *past, own_k = after(key_rows, value_rows, own_k)
     past = [m[:, :local_width] for m in past]
-    past = [lax.ppermute(m, AXES, [(i, i + 1) for i in range(device_count - 1)]) for m in past]
+    onward = [(i, i + 1) for i in range(device_count - 1)]
+    past[0] = lax.ppermute(past[0], AXES, onward)
+    past[1], past[0] = after(past[1], past[0])
+    past[1] = lax.ppermute(past[1], AXES, onward)
     values, own_q = after(values, own_q)
     own_v = one(own_slots, values, "dispatch_values")
     if visitors:

time: 349 us -> 345 us (0.989)
  starting transfers between devices: 60.2 us -> 53.9 us
    ppermute x8, starting transfers between devices: 30.5 us -> 25.1 us  [move(): return lax.ppermute(array, AXES, pairs)]
  transfers between devices with their start and end apart: 17 -> 17, of which waited for: 5 -> 5; matrix products, arithmetic and copies ran while one was open for 3% -> 3% of each run, Pallas kernels for 52% -> 53%
where the time goes in v4:
time: 345 us; the launch traced here: 343 us
  Pallas kernels  188 us (54%)
  waiting for transfers between devices  72.3 us (21%)
  starting transfers between devices  53.9 us (16%)
  between operations  13.8 us (4%)
  local copies, waits for them, and re-layouts  13 us (4%)
    pallas_call x3, Pallas kernels, answer(): pl.pallas_call(functools.partial(answer_kernel, own, steps), grid=(steps...  70.9 us
    pallas_call x5, Pallas kernels, dispatch(): pl.pallas_call(functools.partial(dispatch_kernel, count), grid=(pairs,),...  62.4 us
    all_to_all x6, waiting for transfers between devices, swap(): lax.all_to_all(array, AXES, split_axis=0, concat_axis=0, tiled=True, axis...  47.5 us
    ppermute x8, starting transfers between devices, move(): return lax.ppermute(array, AXES, pairs)  25.1 us
    all_to_all x6, starting transfers between devices, swap(): lax.all_to_all(array, AXES, split_axis=0, concat_axis=0, tiled=True, axis...  24.3 us
    pallas_call x1, Pallas kernels, window_heads(): pl.pallas_call(window_kernel, grid=(HEADS_L,), in_specs=[pl.BlockSpec(mem...  21.7 us
    ppermute x8, waiting for transfers between devices, move(): return lax.ppermute(array, AXES, pairs)  16.2 us
    pallas_call x3, Pallas kernels, heads_first(): pl.pallas_call(heads_kernel, grid=(rows // block,), in_specs=[pl.BlockSpe...  11.8 us
  transfers between devices with their start and end apart: 17, of which 5 were waited for; matrix products, arithmetic and copies ran while one was open for 3% of the time, Pallas kernels for 53%

profile of v4, /device:TPU:24, one launch (start us, length us, event | category | flops | bytes accessed | tf_op | source)
XLA Modules:
  0.0 343.2 jit_solution(4161015862025145535)
XLA Ops:
  6.5 4.0 %heads_first.5 = bf16[8,1024,128]{2,1,0:T(8,128)(2,1)} custom-call(bf16[1024,2048]{1,0:T(8,128)(2,1)} %own_k.1), custom_call_target="tpu_custom_call" | custom-call | tf_op jit(solution)/shard_map/heads_first/pallas_call | solution.py:450
  10.5 3.7 %all-to-all-start = ((bf16[8,1024,128]{2,1,0:T(8,128)(2,1)}), bf16[8,1024,128]{2,1,0:T(8,128)(2,1)S(1)}, u32[]{:S(2)}, u32[]{:S(2)}) async-start(bf16[8,1024,128]{2,1,0:T(8,128)(2,1)} %heads_first.5), calls=%async_computation | async-start | bytes 4194304 | tf_op jit(solution)/shard_map/all_to_all | solution.py:474
  14.2 0.0 all-gather.3.cloned.1.call-start
  14.3 3.9 %heads_first.3 = bf16[8,1024,128]{2,1,0:T(8,128)(2,1)} custom-call(bf16[1024,2048]{1,0:T(8,128)(2,1)} %own_v.1), custom_call_target="tpu_custom_call" | custom-call | tf_op jit(solution)/shard_map/heads_first/pallas_call | solution.py:450
  18.2 6.9 %rank_tokens.1 = (s32[8,1024]{1,0:T(8,128)}, s32[8,256]{1,0:T(8,128)}) custom-call(s32[8,1024]{1,0:T(8,128)} %ids_ref), custom_call_target="tpu_custom_call" | custom-call | tf_op jit(solution)/shard_map/rank_tokens/pallas_call | solution.py:56
  25.1 1.4 pad_add_fusion
  26.5 0.0 all-gather.3.cloned.1.call-update
  26.5 3.9 %heads_first.4 = bf16[8,1024,128]{2,1,0:T(8,128)(2,1)} custom-call(bf16[1024,2048]{1,0:T(8,128)(2,1)} %q_ref.1), custom_call_target="tpu_custom_call" | custom-call | tf_op jit(solution)/shard_map/heads_first/pallas_call | solution.py:450
  30.4 9.8 %all-to-all-done.refs_1_ = bf16[8,1024,128]{2,1,0:T(8,128)(2,1)S(1)} async-done(((bf16[8,1024,128]{2,1,0:T(8,128)(2,1)}), bf16[8,1024,128]{2,1,0:T(8,128)(2,1)S(1)}, u32[]{:S(2)}, u32[]{:S(2)}) %all-to-all-start) | async-done | bytes 2097184 | tf_op jit(solution)/shard_map/all_to_all | solution.py:474
  40.2 4.4 %all-to-all-start.1 = ((bf16[8,1024,128]{2,1,0:T(8,128)(2,1)}), bf16[8,1024,128]{2,1,0:T(8,128)(2,1)}, u32[]{:S(2)}, u32[]{:S(2)}) async-start(bf16[8,1024,128]{2,1,0:T(8,128)(2,1)} %heads_first.4), calls=%async_computation.1 | async-start | bytes 4194304 | tf_op jit(solution)/shard_map/all_to_all | solution.py:474
  44.6 1.3 collective-permute-start
  45.9 25.5 %all-to-all-done.1.refs_0_ = bf16[8,1024,128]{2,1,0:T(8,128)(2,1)} async-done(((bf16[8,1024,128]{2,1,0:T(8,128)(2,1)}), bf16[8,1024,128]{2,1,0:T(8,128)(2,1)}, u32[]{:S(2)}, u32[]{:S(2)}) %all-to-all-start.1) | async-done | bytes 2097184 | tf_op jit(solution)/shard_map/all_to_all | solution.py:474
  71.4 4.4 %all-to-all-start.2 = ((bf16[8,1024,128]{2,1,0:T(8,128)(2,1)}), bf16[8,1024,128]{2,1,0:T(8,128)(2,1)}, u32[]{:S(2)}, u32[]{:S(2)}) async-start(bf16[8,1024,128]{2,1,0:T(8,128)(2,1)} %heads_first.3), calls=%async_computation.2 | async-start | bytes 4194304 | tf_op jit(solution)/shard_map/all_to_all | solution.py:474
  75.9 0.1 lt.76
  76.0 0.6 add_convert_fusion.valid_ref
  76.6 1.3 collective-permute-start.2
  77.9 8.5 %all-gather.3.cloned.1.call-done = s32[256,1280]{1,0:T(8,128)} async-done(((s32[8,1280]{1,0:T(8,128)}), s32[256,1280]{1,0:T(8,128)}) %all-gather.3.cloned.1.call-update) | async-done | bytes 1310736 | tf_op jit(solution)/shard_map/all_gather | solution.py:488
  86.4 1.4 constant_dynamic-slice_fusion
  87.9 0.6 reshape.32.slot_ref
  88.5 0.6 reshape.34.slot_ref
  89.2 0.6 reshape.33.slot_ref
  89.8 2.0 collective-permute-start.1
  91.8 12.7 %dispatch_queries_keys.1 = (bf16[256,4,16,128]{3,2,1,0:T(8,128)(2,1)}, bf16[256,4,16,128]{3,2,1,0:T(8,128)(2,1)}) custom-call(s32[4,2,1024]{2,1,0:T(2,128)} %reshape.32.slot_ref, bf16[8,1024,128]{2,1,0:T(8,128)(2,1)} %all-to-all-done.1.refs_0_, bf16[8,1024,128]{2,1,0:T(8,128)(2,1)} %copy-done.3), custom_call_target="tpu_custom_call" | custom-call | flops 8589934592 | bytes 24000000 | tf_op jit(solution)/shard_map/dispatch_queries_keys/pallas_call | solution.py:139
  104.5 0.0 collective-permute-done
  104.5 0.0 all-to-all-done.2.refs_0_
  104.5 4.4 %all-to-all-start.3 = ((bf16[8,1024,128]{2,1,0:T(8,128)(2,1)}), bf16[8,1024,128]{2,1,0:T(8,128)(2,1)}, u32[]{:S(2)}, u32[]{:S(2)}) async-start(bf16[8,1024,128]{2,1,0:T(8,128)(2,1)} %collective-permute-done), calls=%async_computation.3 | async-start | bytes 4194304 | tf_op jit(solution)/shard_map/all_to_all | solution.py:474
  108.9 0.1 copy.10
  109.0 3.1 slice.33
  112.1 2.3 collective-permute-start.5
  114.4 0.1 copy.9
  114.5 0.6 reshape.35.slot_ref
  115.1 0.0 copy-start
  115.2 12.4 %dispatch_values.1.own_v = bf16[256,4,16,128]{3,2,1,0:T(8,128)(2,1)} custom-call(s32[4,2,1024]{2,1,0:T(2,128)} %reshape.32.slot_ref, bf16[8,1024,128]{2,1,0:T(8,128)(2,1)} %all-to-all-done.2.refs_0_), custom_call_target="tpu_custom_call" | custom-call | flops 4294967296 | bytes 12000000 | tf_op jit(solution)/shard_map/dispatch_values/pallas_call | solution.py:139
  127.6 16.4 %collective-permute-start.3 = (bf16[8,1024,128]{2,1,0:T(8,128)(2,1)}, bf16[8,1024,128]{2,1,0:T(8,128)(2,1)}, u32[]{:S(2)}, u32[]{:S(2)}) collective-permute-start(bf16[8,1024,128]{2,1,0:T(8,128)(2,1)} %all-to-all-done.1.refs_0_), channel_id=1, source_target_pairs={{24,8},{25,9},{26,10},{27,11},{28,12},{29,13},{30,14},{31,15}} | collective-permute-start | bytes 6291464 | tf_op jit(solution)/shard_map/ppermute | solution.py:480
  143.9 0.8 pad_maximum_fusion.bias_ref
  144.7 1.6 slice.32
  146.3 12.2 %dispatch_visit.2.query = bf16[256,4,16,128]{3,2,1,0:T(8,128)(2,1)} custom-call(s32[4,2,1024]{2,1,0:T(2,128)} %reshape.34.slot_ref, bf16[8,1024,128]{2,1,0:T(8,128)(2,1)} %collective-permute-done.1.refs_0_), custom_call_target="tpu_custom_call" | custom-call | flops 4294967296 | bytes 12000000 | tf_op jit(solution)/shard_map/dispatch_visit/pallas_call | solution.py:139
  158.5 0.0 all-to-all-done.3.refs_1_
  158.5 0.0 collective-permute-done.2.refs_0_
  158.5 12.9 %dispatch_pair.1 = (bf16[256,4,16,128]{3,2,1,0:T(8,128)(2,1)}, bf16[256,4,16,128]{3,2,1,0:T(8,128)(2,1)}) custom-call(s32[4,2,1024]{2,1,0:T(2,128)} %reshape.33.slot_ref, bf16[8,1024,128]{2,1,0:T(8,128)(2,1)} %collective-permute-done.2.refs_0_, bf16[8,1024,128]{2,1,0:T(8,128)(2,1)} %all-to-all-done.3.refs_1_), custom_call_target="tpu_custom_call" | custom-call | flops 8589934592 | bytes 24000000 | tf_op jit(solution)/shard_map/dispatch_pair/pallas_call | solution.py:139
  171.4 2.1 collective-permute-start.6
  173.5 23.6 %answer_visit.2 = (bf16[8,528,128]{2,1,0:T(8,128)(2,1)}, bf16[8,528,128]{2,1,0:T(8,128)(2,1)}) custom-call(f32[256,128]{1,0:T(8,128)} %pad_maximum_fusion.bias_ref, bf16[256,4,16,128]{3,2,1,0:T(8,128)(2,1)} %get-tuple-element.65.own_k, bf16[256,4,16,128]{3,2,1,0:T(8,128)(2,1)} %dispatch_values.1.own_v, bf16[256,4,16,128]{3,2,1,0:T(8,128)(2,1)} %get-tuple-element.73.pair_k, ...), custom_call_target="tpu_custom_call" | custom-call | flops 8589934592 | bytes 30000000 | tf_op jit(solution)/shard_map/answer_visit/pallas_call | solution.py:290
  197.1 0.7 collective-permute-start.7
  197.8 12.2 %dispatch_visit.3.query = bf16[256,4,16,128]{3,2,1,0:T(8,128)(2,1)} custom-call(s32[4,2,1024]{2,1,0:T(2,128)} %reshape.35.slot_ref, bf16[8,1024,128]{2,1,0:T(8,128)(2,1)} %collective-permute-done.3.refs_0_), custom_call_target="tpu_custom_call" | custom-call | flops 4294967296 | bytes 12000000 | tf_op jit(solution)/shard_map/dispatch_visit/pallas_call | solution.py:139
  210.0 23.6 %answer_visit.3 = (bf16[8,528,128]{2,1,0:T(8,128)(2,1)}, bf16[8,528,128]{2,1,0:T(8,128)(2,1)}) custom-call(f32[256,128]{1,0:T(8,128)} %pad_maximum_fusion.bias_ref, bf16[256,4,16,128]{3,2,1,0:T(8,128)(2,1)} %get-tuple-element.65.own_k, bf16[256,4,16,128]{3,2,1,0:T(8,128)(2,1)} %dispatch_values.1.own_v, bf16[256,4,16,128]{3,2,1,0:T(8,128)(2,1)} %get-tuple-element.73.pair_k, ...), custom_call_target="tpu_custom_call" | custom-call | flops 8589934592 | bytes 30000000 | tf_op jit(solution)/shard_map/answer_visit/pallas_call | solution.py:290
  233.7 1.3 collective-permute-start.4
  235.0 1.0 collective-permute-start.9
  235.9 23.7 %answer_own.1 = (bf16[8,528,128]{2,1,0:T(8,128)(2,1)}, bf16[8,528,128]{2,1,0:T(8,128)(2,1)}) custom-call(f32[256,128]{1,0:T(8,128)} %pad_maximum_fusion.bias_ref, bf16[256,4,16,128]{3,2,1,0:T(8,128)(2,1)} %get-tuple-element.65.own_k, bf16[256,4,16,128]{3,2,1,0:T(8,128)(2,1)} %dispatch_values.1.own_v, bf16[256,4,16,128]{3,2,1,0:T(8,128)(2,1)} %get-tuple-element.73.pair_k, ...), custom_call_target="tpu_custom_call" | custom-call | flops 8589934592 | bytes 30000000 | tf_op jit(solution)/shard_map/answer_own/pallas_call | solution.py:290
  259.6 0.0 collective-permute-done.7.refs_1_
  259.6 1.3 collective-permute-start.8
  260.9 21.7 %window_heads.1.base_ref = bf16[1024,2048]{1,0:T(8,128)(2,1)} custom-call(s32[1]{0:T(128)} %bitcast.9.first_ref, bf16[1024,2048]{1,0:T(8,128)(2,1)} %q_ref.1, bf16[1024,2048]{1,0:T(8,128)(2,1)} %own_k.1, bf16[1024,2048]{1,0:T(8,128)(2,1)} %own_v.1, bf16[1024,1024]{1,0:T(8,128)(2,1)} %collective-permute-done.5.past_k, ...), custom_call_target="tpu_custom_call" | custom-call | flops 10737418240 | bytes 14000000 | tf_op jit(solution)/shard_map/window_heads/pallas_call | solution.py:356
  282.7 0.0 collective-permute-done.9.refs_1_
  282.7 1.0 copy-done.6
  283.7 1.0 copy-done.7
  284.7 4.7 %merge_parts.3 = bf16[8,512,128]{2,1,0:T(8,128)(2,1)} custom-call(s32[3]{0:T(128)} %add_convert_fusion.valid_ref, bf16[8,528,128]{2,1,0:T(8,128)(2,1)} %get-tuple-element.94.refs_0_, bf16[8,528,128]{2,1,0:T(8,128)(2,1)} %copy-done.7, bf16[8,528,128]{2,1,0:T(8,128)(2,1)} %copy-done.6), custom_call_target="tpu_custom_call" | custom-call | tf_op jit(solution)/shard_map/merge_parts/pallas_call | solution.py:405
  289.4 3.9 %all-to-all-start.4 = ((bf16[8,512,128]{2,1,0:T(8,128)(2,1)}), bf16[8,512,128]{2,1,0:T(8,128)(2,1)S(1)}, u32[]{:S(2)}, u32[]{:S(2)}) async-start(bf16[8,512,128]{2,1,0:T(8,128)(2,1)} %merge_parts.3), calls=%async_computation.4 | async-start | bytes 2097152 | tf_op jit(solution)/shard_map/all_to_all | solution.py:474
  293.3 16.2 %collective-permute-done.8.refs_2_ = bf16[8,528,128]{2,1,0:T(8,128)(2,1)S(1)} collective-permute-done((bf16[8,528,128]{2,1,0:T(8,128)(2,1)}, bf16[8,528,128]{2,1,0:T(8,128)(2,1)S(1)}, u32[]{:S(2)}, u32[]{:S(2)}) %collective-permute-start.8) | collective-permute-done | bytes 1081376 | tf_op jit(solution)/shard_map/ppermute | solution.py:480
  309.5 1.0 copy-done.8
  310.5 4.7 %merge_parts.2 = bf16[8,512,128]{2,1,0:T(8,128)(2,1)} custom-call(s32[3]{0:T(128)} %add_convert_fusion.valid_ref, bf16[8,528,128]{2,1,0:T(8,128)(2,1)} %get-tuple-element.89.refs_0_, bf16[8,528,128]{2,1,0:T(8,128)(2,1)} %copy-done.5, bf16[8,528,128]{2,1,0:T(8,128)(2,1)} %copy-done.8), custom_call_target="tpu_custom_call" | custom-call | tf_op jit(solution)/shard_map/merge_parts/pallas_call | solution.py:405
  315.2 3.6 %all-to-all-start.5 = ((bf16[8,512,128]{2,1,0:T(8,128)(2,1)}), bf16[8,512,128]{2,1,0:T(8,128)(2,1)S(1)}, u32[]{:S(2)}, u32[]{:S(2)}) async-start(bf16[8,512,128]{2,1,0:T(8,128)(2,1)} %merge_parts.2), calls=%async_computation.5 | async-start | bytes 2097152 | tf_op jit(solution)/shard_map/all_to_all | solution.py:474
  318.8 2.2 place_heads.2.base_ref
  321.0 12.2 %all-to-all-done.5.heads_ref = bf16[8,512,128]{2,1,0:T(8,128)(2,1)S(1)} async-done(((bf16[8,512,128]{2,1,0:T(8,128)(2,1)}), bf16[8,512,128]{2,1,0:T(8,128)(2,1)S(1)}, u32[]{:S(2)}, u32[]{:S(2)}) %all-to-all-start.5) | async-done | bytes 1048608 | tf_op jit(solution)/shard_map/all_to_all | solution.py:474
  333.2 1.0 copy-done.2
  334.2 2.2 place_heads.3
  (32 shorter events, 0.1 us)
Async XLA Ops:
  10.5 29.7 %all-to-all-start = ((bf16[8,1024,128]{2,1,0:T(8,128)(2,1)}), bf16[8,1024,128]{2,1,0:T(8,128)(2,1)S(1)}, u32[]{:S(2)}, u32[]{:S(2)}) async-start(bf16[8,1024,128]{2,1,0:T(8,128)(2,1)} %heads_first.5), calls=%async_computation | async-start | bytes 4194304 | tf_op jit(solution)/shard_map/all_to_all | solution.py:474
  14.2 72.2 %all-gather.3.cloned.1.call-start = ((), (), s32[]{:S(2)}) async-start(), calls=%async_computation.6 | async-start | bytes 1351680 | tf_op jit(solution)/shard_map/all_gather | solution.py:488
  40.2 36.4 %copy-start.3 = (bf16[8,1024,128]{2,1,0:T(8,128)(2,1)}, bf16[8,1024,128]{2,1,0:T(8,128)(2,1)S(1)}, u32[]{:S(2)}) copy-start(bf16[8,1024,128]{2,1,0:T(8,128)(2,1)S(1)} %all-to-all-done.refs_1_) | copy-start | bytes 6291460
  40.2 31.2 %all-to-all-start.1 = ((bf16[8,1024,128]{2,1,0:T(8,128)(2,1)}), bf16[8,1024,128]{2,1,0:T(8,128)(2,1)}, u32[]{:S(2)}, u32[]{:S(2)}) async-start(bf16[8,1024,128]{2,1,0:T(8,128)(2,1)} %heads_first.4), calls=%async_computation.1 | async-start | bytes 4194304 | tf_op jit(solution)/shard_map/all_to_all | solution.py:474
  44.6 59.9 %collective-permute-start = (bf16[8,1024,128]{2,1,0:T(8,128)(2,1)}, bf16[8,1024,128]{2,1,0:T(8,128)(2,1)}, u32[]{:S(2)}, u32[]{:S(2)}) collective-permute-start(bf16[8,1024,128]{2,1,0:T(8,128)(2,1)} %heads_first.3), channel_id=1, source_target_pairs={{0,8},{1,9},{2,10},{3,11},{4,12},{5,13},{6,14},{7,15},{16,24},{17,... | collective-permute-start | bytes 6291464 | tf_op jit(solution)/shard_map/ppermute | solution.py:480
  71.4 33.1 %all-to-all-start.2 = ((bf16[8,1024,128]{2,1,0:T(8,128)(2,1)}), bf16[8,1024,128]{2,1,0:T(8,128)(2,1)}, u32[]{:S(2)}, u32[]{:S(2)}) async-start(bf16[8,1024,128]{2,1,0:T(8,128)(2,1)} %heads_first.3), calls=%async_computation.2 | async-start | bytes 4194304 | tf_op jit(solution)/shard_map/all_to_all | solution.py:474
  76.6 81.9 %collective-permute-start.2 = (bf16[8,1024,128]{2,1,0:T(8,128)(2,1)S(1)}, bf16[8,1024,128]{2,1,0:T(8,128)(2,1)}, u32[]{:S(2)}, u32[]{:S(2)}) collective-permute-start(bf16[8,1024,128]{2,1,0:T(8,128)(2,1)S(1)} %all-to-all-done.refs_1_), channel_id=1, source_target_pairs={{0,8},{1,9},{2,10},{3,11},{4,12},{5,13},{6,14},{7,15},{16,24},{17,... | collective-permute-start | bytes 6291464 | tf_op jit(solution)/shard_map/ppermute | solution.py:480
  89.8 37.8 %collective-permute-start.1 = (bf16[8,1024,128]{2,1,0:T(8,128)(2,1)}, bf16[8,1024,128]{2,1,0:T(8,128)(2,1)}, u32[]{:S(2)}, u32[]{:S(2)}) collective-permute-start(bf16[8,1024,128]{2,1,0:T(8,128)(2,1)} %all-to-all-done.1.refs_0_), channel_id=1, source_target_pairs={{16,8},{17,9},{18,10},{19,11},{20,12},{21,13},{22,14},{23,15}} | collective-permute-start | bytes 6291464 | tf_op jit(solution)/shard_map/ppermute | solution.py:480
  104.5 54.0 %all-to-all-start.3 = ((bf16[8,1024,128]{2,1,0:T(8,128)(2,1)}), bf16[8,1024,128]{2,1,0:T(8,128)(2,1)}, u32[]{:S(2)}, u32[]{:S(2)}) async-start(bf16[8,1024,128]{2,1,0:T(8,128)(2,1)} %collective-permute-done), calls=%async_computation.3 | async-start | bytes 4194304 | tf_op jit(solution)/shard_map/all_to_all | solution.py:474
  112.1 59.3 %collective-permute-start.5 = (bf16[1024,1024]{1,0:T(8,128)(2,1)}, bf16[1024,1024]{1,0:T(8,128)(2,1)}, u32[]{:S(2)}, u32[]{:S(2)}) collective-permute-start(bf16[1024,1024]{1,0:T(8,128)(2,1)} %slice.33), channel_id=1, source_target_pairs={{0,1},{1,2},{2,3},{3,4},{4,5},{5,6},{6,7},{7,8},{8,9},{9,10},{10,1... | collective-permute-start | bytes 6291464 | tf_op jit(solution)/shard_map/ppermute | solution.py:539
  115.1 29.6 %copy-start = (bf16[1024,2048]{1,0:T(8,128)(2,1)S(1)}, bf16[1024,2048]{1,0:T(8,128)(2,1)}, u32[]{:S(2)}) copy-start(bf16[1024,2048]{1,0:T(8,128)(2,1)} %own_v.1) | copy-start | bytes 12582916
  127.6 70.2 %collective-permute-start.3 = (bf16[8,1024,128]{2,1,0:T(8,128)(2,1)}, bf16[8,1024,128]{2,1,0:T(8,128)(2,1)}, u32[]{:S(2)}, u32[]{:S(2)}) collective-permute-start(bf16[8,1024,128]{2,1,0:T(8,128)(2,1)} %all-to-all-done.1.refs_0_), channel_id=1, source_target_pairs={{24,8},{25,9},{26,10},{27,11},{28,12},{29,13},{30,14},{31,15}} | collective-permute-start | bytes 6291464 | tf_op jit(solution)/shard_map/ppermute | solution.py:480
  158.5 12.9 %copy-start.4 = (bf16[1024,1024]{1,0:T(8,128)(2,1)S(1)}, bf16[1024,1024]{1,0:T(8,128)(2,1)}, u32[]{:S(2)}) copy-start(bf16[1024,1024]{1,0:T(8,128)(2,1)} %slice.32) | copy-start | bytes 6291460
  171.4 89.6 %collective-permute-start.6 = (bf16[1024,1024]{1,0:T(8,128)(2,1)S(1)}, bf16[1024,1024]{1,0:T(8,128)(2,1)}, u32[]{:S(2)}, u32[]{:S(2)}) collective-permute-start(bf16[1024,1024]{1,0:T(8,128)(2,1)S(1)} %copy-done.4), channel_id=1, source_target_pairs={{0,1},{1,2},{2,3},{3,4},{4,5},{5,6},{6,7},{7,8},{8,9},{9,10},{10,1... | collective-permute-start | bytes 6291464 | tf_op jit(solution)/shard_map/ppermute | solution.py:541
  197.1 62.5 %collective-permute-start.7 = (bf16[8,528,128]{2,1,0:T(8,128)(2,1)}, bf16[8,528,128]{2,1,0:T(8,128)(2,1)S(1)}, u32[]{:S(2)}, u32[]{:S(2)}) collective-permute-start(bf16[8,528,128]{2,1,0:T(8,128)(2,1)} %get-tuple-element.91), channel_id=1, source_target_pairs={{8,16},{9,17},{10,18},{11,19},{12,20},{13,21},{14,22},{15,23}} | collective-permute-start | bytes 3244040 | tf_op jit(solution)/shard_map/ppermute | solution.py:480
  210.0 24.9 %copy-start.9 = (bf16[8,528,128]{2,1,0:T(8,128)(2,1)S(1)}, bf16[8,528,128]{2,1,0:T(8,128)(2,1)}, u32[]{:S(2)}) copy-start(bf16[8,528,128]{2,1,0:T(8,128)(2,1)} %get-tuple-element.95) | copy-start | bytes 3244036
  233.7 49.0 %collective-permute-start.4 = (bf16[8,528,128]{2,1,0:T(8,128)(2,1)}, bf16[8,528,128]{2,1,0:T(8,128)(2,1)S(1)}, u32[]{:S(2)}, u32[]{:S(2)}) collective-permute-start(bf16[8,528,128]{2,1,0:T(8,128)(2,1)} %get-tuple-element.80), channel_id=1, source_target_pairs={{8,24},{9,25},{10,26},{11,27},{12,28},{13,29},{14,30},{15,31}} | collective-permute-start | bytes 3244040 | tf_op jit(solution)/shard_map/ppermute | solution.py:480
  235.0 47.7 %collective-permute-start.9 = (bf16[8,528,128]{2,1,0:T(8,128)(2,1)S(1)}, bf16[8,528,128]{2,1,0:T(8,128)(2,1)S(1)}, u32[]{:S(2)}, u32[]{:S(2)}) collective-permute-start(bf16[8,528,128]{2,1,0:T(8,128)(2,1)S(1)} %copy-done.9), channel_id=1, source_target_pairs={{8,16},{9,17},{10,18},{11,19},{12,20},{13,21},{14,22},{15,23}} | collective-permute-start | bytes 3244040 | tf_op jit(solution)/shard_map/ppermute | solution.py:480
  259.6 23.0 %copy-start.5 = (bf16[8,528,128]{2,1,0:T(8,128)(2,1)}, bf16[8,528,128]{2,1,0:T(8,128)(2,1)S(1)}, u32[]{:S(2)}) copy-start(bf16[8,528,128]{2,1,0:T(8,128)(2,1)S(1)} %collective-permute-done.7.refs_1_) | copy-start | bytes 3244036
  259.6 49.9 %collective-permute-start.8 = (bf16[8,528,128]{2,1,0:T(8,128)(2,1)}, bf16[8,528,128]{2,1,0:T(8,128)(2,1)S(1)}, u32[]{:S(2)}, u32[]{:S(2)}) collective-permute-start(bf16[8,528,128]{2,1,0:T(8,128)(2,1)} %get-tuple-element.93), channel_id=1, source_target_pairs={{8,24},{9,25},{10,26},{11,27},{12,28},{13,29},{14,30},{15,31}} | collective-permute-start | bytes 3244040 | tf_op jit(solution)/shard_map/ppermute | solution.py:480
  282.7 1.0 copy-start.6
  283.7 1.0 copy-start.7
  289.4 25.8 %all-to-all-start.4 = ((bf16[8,512,128]{2,1,0:T(8,128)(2,1)}), bf16[8,512,128]{2,1,0:T(8,128)(2,1)S(1)}, u32[]{:S(2)}, u32[]{:S(2)}) async-start(bf16[8,512,128]{2,1,0:T(8,128)(2,1)} %merge_parts.3), calls=%async_computation.4 | async-start | bytes 2097152 | tf_op jit(solution)/shard_map/all_to_all | solution.py:474
  309.5 1.0 copy-start.8
  315.2 3.6 %copy-start.1 = (bf16[8,512,128]{2,1,0:T(8,128)(2,1)}, bf16[8,512,128]{2,1,0:T(8,128)(2,1)S(1)}, u32[]{:S(2)}) copy-start(bf16[8,512,128]{2,1,0:T(8,128)(2,1)S(1)} %all-to-all-done.4.heads_ref) | copy-start | bytes 3145732
  315.2 18.0 %all-to-all-start.5 = ((bf16[8,512,128]{2,1,0:T(8,128)(2,1)}), bf16[8,512,128]{2,1,0:T(8,128)(2,1)S(1)}, u32[]{:S(2)}, u32[]{:S(2)}) async-start(bf16[8,512,128]{2,1,0:T(8,128)(2,1)} %merge_parts.2), calls=%async_computation.5 | async-start | bytes 2097152 | tf_op jit(solution)/shard_map/all_to_all | solution.py:474
  333.2 1.0 copy-start.2
Sparse Core Ops, SparseCore 0:
  26.6 59.7 all-gather.2
